TPU v7x, 512 devices: a whole 4x4x16 slice. The times are simulated.
512 devices in a mesh: seq: 64 (over x, z), chan: 8 (over y, core).
Axes of the slice: x: 4, y: 4, z: 16, core: 2. Of those that a mesh axis runs over, the one named last changes fastest.
Arguments:
- signal: bfloat16 [16384, 8192], P('seq', 'chan'), parts along dimension 1, may hold values from -6 to 6
- cotangent: bfloat16 [16384, 8192], P('seq', 'chan'), parts along dimension 1, may hold values from -6 to 6
- decay_rate: float32 [16, 8192], P(None, 'chan'), parts along dimension 1, may hold values from 1.2207031e-05 to 0.0333333333
- residue: float32 [16, 8192], P(None, 'chan'), parts along dimension 1, may hold values from -1.5 to 1.5
- skip_gain: float32 [8192], P('chan'), parts along dimension 0, may hold values from 0.5 to 1.5
Outputs:
- output: bfloat16 [16384, 8192], P('seq', 'chan'), parts along dimension 1
- grad_signal: bfloat16 [16384, 8192], P('seq', 'chan'), parts along dimension 1
There are 8 independent parts, one for each index of `chan`. A program takes and returns all parts, laid end to end along the dimension named above; each array names one. Nothing has to cross between parts.
All inputs are finite; a program needn't handle non-finite values.
Results may differ from a plain program's by a relative error of at most 0.007.
Values sent between devices are 32-bit elements; how exact they have to be, the bound alone decides.
No kernel may reach another device: no remote copies, remote signals or barrier semaphores. Data moves between devices by JAX's collectives and lax.ppermute only.
A program may use at most 128 MiB of HBM per device.

v0:
```python
import jax
import jax.numpy as jnp
from jax import lax
from jax.sharding import PartitionSpec as P

BLOCK = 32


def shifted(x, axis, by):
    peers = lax.axis_size(axis)
    pairs = [(i, i + by) for i in range(peers) if 0 <= i + by < peers]
    return lax.ppermute(x, axis, pairs)


def build_tables(decay_rate, residue, block_rows):
    positions = jnp.arange(block_rows, dtype=jnp.float32)
    weight = residue * jnp.sqrt(-jnp.expm1(-2.0 * decay_rate))
    decays = jnp.exp(-decay_rate[:, None, :] * positions[None, :, None])
    filter_taps = jnp.sum(weight[:, None, :] * decays, axis=0)
    lag_index = (
        jnp.arange(block_rows, dtype=jnp.int32)[:, None]
        - jnp.arange(block_rows, dtype=jnp.int32)[None, :]
    )
    picked = jnp.take(filter_taps, jnp.clip(lag_index, 0, block_rows - 1), axis=0)
    toeplitz = jnp.where((lag_index >= 0)[:, :, None], picked, jnp.float32(0.0))
    tail_decay = jnp.flip(decays, axis=1)
    readout = weight[:, None, :] * jnp.exp(
        -decay_rate[:, None, :] * (positions + 1.0)[None, :, None]
    )
    return (toeplitz, tail_decay, readout)


def split_table(table):
    upper = table.astype(jnp.bfloat16)
    lower = (table - upper.astype(jnp.float32)).astype(jnp.bfloat16)
    return (upper, lower)


def split_product(form, table_parts, blocks):
    first = jnp.einsum(form, table_parts[0], blocks, preferred_element_type=jnp.float32)
    second = jnp.einsum(form, table_parts[1], blocks, preferred_element_type=jnp.float32)
    return first + second


def carry_states(device_end, span_rate, forward):
    span_decay = jnp.exp(-span_rate)
    seq_count = lax.axis_size("seq")

    def relay_turn(turn_index, incoming):
        outgoing = span_decay * incoming + device_end
        if forward:
            return shifted(outgoing, "seq", 1)
        return shifted(outgoing, "seq", -1)

    return lax.fori_loop(0, seq_count - 1, relay_turn, jnp.zeros_like(device_end))


def evaluate(signal, decay_rate, tables, skip_gain, forward):
    toeplitz_parts, tail_parts, readout = tables
    block_rows = readout.shape[1]
    channels = signal.shape[1]
    blocks = signal.reshape(-1, block_rows, channels)
    block_count = blocks.shape[0]
    within = split_product("tsc,bsc->btc", toeplitz_parts, blocks)
    block_ends = split_product("nsc,bsc->bnc", tail_parts, blocks)
    block_decay = jnp.exp(-decay_rate * block_rows)

    def advance(state_now, block_end):
        return (block_decay * state_now + block_end, state_now)

    device_end, entering = lax.scan(advance, jnp.zeros(decay_rate.shape, jnp.float32), block_ends)
    incoming = carry_states(device_end, decay_rate * float(block_rows * block_count), forward)
    starts = (block_rows * jnp.arange(block_count, dtype=jnp.float32))[:, None, None]
    powers = jnp.exp(-decay_rate[None, :, :] * starts)
    entering = entering + powers * incoming[None, :, :]
    carried = jnp.einsum("ntc,bnc->btc", readout, entering, precision=lax.Precision.HIGHEST)
    total = within + carried + skip_gain[None, None, :] * blocks.astype(jnp.float32)
    return total.reshape(-1, channels).astype(jnp.bfloat16)


def shards(signal, cotangent, decay_rate, residue, skip_gain):
    toeplitz, tail_decay, readout = build_tables(decay_rate, residue, BLOCK)
    tables = (split_table(toeplitz), split_table(tail_decay), readout)
    output = evaluate(signal, decay_rate, tables, skip_gain, True)
    reversed_grad = evaluate(jnp.flip(cotangent, 0), decay_rate, tables, skip_gain, False)
    grad_signal = jnp.flip(reversed_grad, 0)
    return (output, grad_signal)


def solution(mesh):
    in_specs = (P("seq", "chan"), P("seq", "chan"), P(None, "chan"), P(None, "chan"), P("chan"))
    out_specs = (P("seq", "chan"), P("seq", "chan"))
    return jax.shard_map(shards, mesh=mesh, in_specs=in_specs, out_specs=out_specs, check_vma=False)
```

profile of v0, /device:TPU:6, one launch (start us, length us, event | category | flops | bytes accessed | tf_op | source)
XLA Modules:
  0.0 1286.0 jit_solution(15374921428489532374)
XLA Ops:
  2.0 13.1 %multiply_reduce_fusion = (f32[32,1024]{0,1:T(8,128)S(1)}, f32[16,32,1024]{1,0,2:T(8,128)}) fusion(f32[16,1024]{0,1:T(8,128)S(1)} %copy.57, f32[16,1024]{0,1:T(8,128)S(1)} %copy.58), kind=kLoop, calls=%fused_computation.14 | loop fusion | flops 1540096 | bytes 2359296 | tf_op jit(solution)/shard_map/reduce_sum | solution.py:19
  15.1 13.2 %rev.11 = f32[16,32,1024]{1,0,2:T(8,128)} reverse(f32[16,32,1024]{1,0,2:T(8,128)} %get-tuple-element.223), dimensions={1} | reverse | bytes 4194304 | tf_op jit(solution)/shard_map/jit(_flip)/rev | solution.py:26
  43.7 7.3 while.48
  51.0 530.9 %while.46 = (s32[]{:T(128)}, f32[16,1024]{1,0:T(8,128)S(1)}, f32[16,1024]{1,0:T(8,128)S(1)}, f32[16,1024]{1,0:T(8,128)S(1)}, s32[]{:T(128)}) while((s32[]{:T(128)}, f32[16,1024]{1,0:T(8,128)S(1)}, f32[16,1024]{1,0:T(8,128)S(1)}, f32[16,1024]{1,0:T(8,128)S(1)}, s32[]{:T(128)}) %tuple.94), condition=%wide.region_4.5_spmd, body=%wide.region_3.4_spmd.sunk | while | flops 32770 | bytes 524389 | solution.py:55
  54.9 10.1 collective-permute-done
  100.0 6.6 collective-permute-done
  158.3 6.9 collective-permute-done
  208.6 6.7 collective-permute-done
  258.7 6.5 collective-permute-done
  316.9 7.0 collective-permute-done
  367.3 6.6 collective-permute-done
  425.7 6.5 collective-permute-done
  475.6 7.0 collective-permute-done
  597.2 10.3 add_bitcast_fusion
  611.8 12.2 while.49
  624.1 521.0 %while.47 = (s32[]{:T(128)}, f32[16,1024]{1,0:T(8,128)S(1)}, f32[16,1024]{1,0:T(8,128)S(1)}, f32[16,1024]{1,0:T(8,128)S(1)}, s32[]{:T(128)}) while((s32[]{:T(128)}, f32[16,1024]{1,0:T(8,128)S(1)}, f32[16,1024]{1,0:T(8,128)S(1)}, f32[16,1024]{1,0:T(8,128)S(1)}, s32[]{:T(128)}) %tuple.97), condition=%wide.region_8.9_spmd, body=%wide.region_7.8_spmd.sunk | while | flops 32770 | bytes 524389 | solution.py:55
  678.5 6.5 collective-permute-start.1
  728.4 6.5 collective-permute-start.1
  787.1 6.5 collective-permute-start.1
  837.1 6.5 collective-permute-start.1
  887.0 6.5 collective-permute-start.1
  895.4 6.5 collective-permute-start.1
  945.7 6.5 collective-permute-start.1
  995.7 6.5 collective-permute-start.1
  1151.1 13.2 %fusion.2 = f32[1024,8,32]{2,1,0:T(8,128)} fusion(f32[8,16,1024]{1,0,2:T(8,128)} %copy.68, f32[32]{0:T(128)S(1)} %iota_add_fusion, f32[16,1024]{0,1:T(8,128)} %copy-done.4, f32[16,1024]{0,1:T(8,128)} %copy-done.5), kind=kOutput, calls=%fused_computation.12 | convolution fusion | flops 51380224 | bytes 1704064 | tf_op jit(solution)/shard_map/ntc,bnc->btc/dot_general | solution.py:76
  1171.6 13.2 %fusion.1 = f32[1024,8,32]{2,1,0:T(8,128)} fusion(f32[8,16,1024]{1,0,2:T(8,128)} %copy.77, f32[32]{0:T(128)S(1)} %iota_add_fusion, f32[16,1024]{0,1:T(8,128)} %copy-done.4, f32[16,1024]{0,1:T(8,128)} %copy-done.5), kind=kOutput, calls=%fused_computation.11 | convolution fusion | flops 51380224 | bytes 1704064 | tf_op jit(solution)/shard_map/ntc,bnc->btc/dot_general | solution.py:76
  1194.2 14.3 %copy.60 = f32[32,32,1024]{1,0,2:T(8,128)} copy(f32[32,32,1024]{2,1,0:T(8,128)} %bitcast.53) | data formatting | bytes 8388608 | tf_op jit(solution)/shard_map/jit(_take)/gather | solution.py:24
  1208.6 12.7 fusion.3
  1225.1 12.8 fusion.29
  1241.5 12.1 fusion.5
  1257.3 12.2 fusion.30
  1277.3 8.3 rev.13
  (448 shorter events, 1030.9 us)
Async XLA Ops:
  51.1 13.9 %collective-permute-start = (f32[16,1024]{1,0:T(8,128)S(1)}, f32[16,1024]{1,0:T(8,128)S(1)}, u32[]{:S(2)}, u32[]{:S(2)}) collective-permute-start(f32[16,1024]{1,0:T(8,128)S(1)} %multiply_add_fusion.6), channel_id=1, source_target_pairs={{0,8},{8,16},{16,24},{24,32},{32,40},{40,48},{48,56},{56,64},{64,7... | collective-permute-start | bytes 196616 | tf_op jit(solution)/shard_map/while/body/eval_jaxpr/ppermute | solution.py:12
  98.1 8.5 collective-permute-start
  106.6 8.3 collective-permute-start
  156.4 8.9 collective-permute-start
  206.7 8.6 collective-permute-start
  256.8 8.4 collective-permute-start
  265.2 8.4 collective-permute-start
  315.0 8.9 collective-permute-start
  365.4 8.5 collective-permute-start
  415.4 8.4 collective-permute-start
  423.7 8.4 collective-permute-start
  473.6 8.9 collective-permute-start
  645.1 8.3 collective-permute-start.1
  661.7 8.3 collective-permute-start.1
  670.0 8.5 collective-permute-start.1
  678.5 8.4 collective-permute-start.1
  695.2 8.3 collective-permute-start.1
  711.8 8.3 collective-permute-start.1
  720.0 8.3 collective-permute-start.1
  728.4 8.4 collective-permute-start.1
  736.8 8.3 collective-permute-start.1
  778.3 8.8 collective-permute-start.1
  787.1 8.4 collective-permute-start.1
  828.7 8.4 collective-permute-start.1
  837.1 8.4 collective-permute-start.1
  887.0 8.4 collective-permute-start.1
  895.4 8.4 collective-permute-start.1
  936.9 8.8 collective-permute-start.1
  945.7 8.4 collective-permute-start.1
  987.3 8.4 collective-permute-start.1
  995.7 8.4 collective-permute-start.1
  1004.1 8.3 collective-permute-start.1
  (104 other events, 1371.5 us)
where the time goes:
time: 1300 us; the launch traced here: 1290 us
  waiting for transfers between devices  529 us (41%)
  starting transfers between devices  520 us (40%)
  matrix products  103 us (8%)
  local copies, waits for them, and re-layouts  89.6 us (7%)
  other arithmetic  41.4 us (3%)
    ppermute x126, waiting for transfers between devices, shifted(): return lax.ppermute(x, axis, pairs)  529 us
    ppermute x126, starting transfers between devices, shifted(): return lax.ppermute(x, axis, pairs)  520 us
    dot_general x4, matrix products, split_product(): jnp.einsum(form, table_parts[1], blocks, preferred_element_type=jnp.float32)  39.5 us
    dot_general x4, matrix products, split_product(): jnp.einsum(form, table_parts[0], blocks, preferred_element_type=jnp.float32)  37.1 us
    dot_general x2, matrix products, evaluate(): jnp.einsum('ntc,bnc->btc', readout, entering, precision=lax.Precision.HIG...  26.5 us
  transfers between devices with their start and end apart: 126, of which 126 were waited for; matrix products, arithmetic and copies ran while one was open for 0% of the time, Pallas kernels for 0%

commit v1 on v0

v1 whole, which is shorter than its diff:
```python
import functools
import jax
import jax.numpy as jnp
from jax import lax
from jax.experimental import pallas as pl
from jax.experimental.pallas import tpu as pltpu
from jax.sharding import PartitionSpec as P

SUB = 8
LANES = 128
F32 = jnp.float32


def row_of(table, n):
    return jnp.broadcast_to(table[n : n + 1, :], (SUB, LANES))


def block_index():
    return lax.broadcasted_iota(jnp.int32, (SUB, LANES), 0)


def blocked_position(x_ref, r, length):
    return x_ref[pl.ds(r, SUB, stride=length), :]


def block_ends(x_ref, decay, order, length):
    ends = [None] * len(decay)
    for step, r in enumerate(order):
        x = blocked_position(x_ref, r, length)
        for n in range(len(decay)):
            ends[n] = x if step == 0 else decay[n] * ends[n] + x
    return ends


def orders(length):
    return list(range(length)), list(range(length - 1, -1, -1))


def ends_kernel(signal_ref, cotangent_ref, rate_ref, ends_ref, span_ref, x_ref, g_ref):
    positions = signal_ref.shape[0]
    length = positions // SUB
    states = rate_ref.shape[0]
    x_ref[...] = signal_ref[...].astype(F32)
    g_ref[...] = cotangent_ref[...].astype(F32)
    rate = rate_ref[...]
    span_ref[...] = jnp.exp(-rate * float(positions))
    decay_table = jnp.exp(-rate)
    decay = [row_of(decay_table, n) for n in range(states)]
    block = block_index()
    forward, backward = orders(length)
    later = (length * (SUB - 1 - block)).astype(F32)
    earlier = (length * block).astype(F32)
    for side, (ref, order, distance) in enumerate(
        ((x_ref, forward, later), (g_ref, backward, earlier))
    ):
        ends = block_ends(ref, decay, order, length)
        for n in range(states):
            scaled = jnp.exp(-row_of(rate, n) * distance) * ends[n]
            ends_ref[side, n : n + 1, :] = jnp.sum(scaled, axis=0, keepdims=True)


def entering_states(ends, rate, length, forward):
    block = block_index()
    entering = []
    for n in range(len(ends)):
        total = ends[n]
        reach = 1
        while reach < SUB:
            ratio = jnp.exp(-row_of(rate, n) * float(length * reach))
            total = total + ratio * shifted_blocks(total, reach, block, forward)
            reach *= 2
        entering.append(shifted_blocks(total, 1, block, forward))
    return entering


def shifted_blocks(x, by, block, forward):
    if forward:
        return jnp.where(block >= by, pltpu.roll(x, by, 0), 0.0)
    return jnp.where(block < SUB - by, pltpu.roll(x, SUB - by, 0), 0.0)


def within_kernel(
    signal_ref, cotangent_ref, rate_ref, weight_ref, gain_ref, y_ref, z_ref, x_ref, g_ref
):
    positions = signal_ref.shape[0]
    length = positions // SUB
    states = rate_ref.shape[0]
    x_ref[...] = signal_ref[...].astype(F32)
    g_ref[...] = cotangent_ref[...].astype(F32)
    rate = rate_ref[...]
    decay_table = jnp.exp(-rate)
    decay = [row_of(decay_table, n) for n in range(states)]
    weight_table = weight_ref[...]
    weight = [row_of(weight_table, n) for n in range(states)]
    gain = jnp.broadcast_to(gain_ref[...], (SUB, LANES))
    forward, backward = orders(length)
    for ref, out_ref, order in ((x_ref, y_ref, forward), (g_ref, z_ref, backward)):
        ends = block_ends(ref, decay, order, length)
        state = entering_states(ends, rate, length, order[0] == 0)
        for r in order:
            x = blocked_position(ref, r, length)
            terms = [gain * x]
            for n in range(states):
                state[n] = decay[n] * state[n] + x
                terms.append(weight[n] * state[n])
            out_ref[r * SUB : (r + 1) * SUB, :] = added(terms)


def added(terms):
    while len(terms) > 1:
        terms = [
            terms[i] + terms[i + 1] if i + 1 < len(terms) else terms[i]
            for i in range(0, len(terms), 2)
        ]
    return terms[0]


def relay_kernel(share_ref, ends_ref, span_ref, carried_ref):
    devices, rows, _ = ends_ref.shape
    share = share_ref[0]
    forward = share < devices // 2
    start = lax.rem(share, devices // 2) * rows
    span = span_ref[pl.ds(start, rows), :]
    state = jnp.zeros(span.shape, F32)
    for step in range(devices):
        at = jnp.where(forward, step, devices - 1 - step)
        end = ends_ref[at]
        carried_ref[at] = state
        state = span * state + end


def carry_kernel(y_ref, z_ref, rate_ref, weight_ref, carried_ref, out_ref, grad_ref, a_ref, b_ref):
    positions = y_ref.shape[0]
    length = positions // SUB
    states = rate_ref.shape[0]
    rate = rate_ref[...]
    decay_table = jnp.exp(-rate)
    decay = [row_of(decay_table, n) for n in range(states)]
    weight = weight_ref[...]
    block = block_index()
    forward, backward = orders(length)
    after_start = (length * block + 1).astype(F32)
    before_end = (length * (SUB - 1 - block) + 1).astype(F32)
    for side, (ref, scratch, result, order, distance) in enumerate(
        (
            (y_ref, a_ref, out_ref, forward, after_start),
            (z_ref, b_ref, grad_ref, backward, before_end),
        )
    ):
        scaled = weight * carried_ref[side]
        terms = [
            jnp.exp(-row_of(rate, n) * distance) * row_of(scaled, n) for n in range(states)
        ]
        for step, r in enumerate(order):
            if step:
                terms = [decay[n] * terms[n] for n in range(states)]
            total = added(terms + [ref[r * SUB : (r + 1) * SUB, :]])
            scratch[pl.ds(r, SUB, stride=length), :] = total
        result[...] = scratch[...].astype(result.dtype)


def shards(signal, cotangent, decay_rate, residue, skip_gain):
    positions, channels = signal.shape
    states = decay_rate.shape[0]
    columns = channels // LANES
    devices = lax.axis_size("seq")
    grid = (columns,)
    wide = pl.BlockSpec((positions, LANES), lambda c: (0, c))
    state_wide = pl.BlockSpec((states, LANES), lambda c: (0, c))
    one_wide = pl.BlockSpec((1, LANES), lambda c: (0, c))
    stacked = pl.BlockSpec((2, states, LANES), lambda c: (0, c, 0))
    scratch = [pltpu.VMEM((positions, LANES), F32)] * 2
    pair = [jax.ShapeDtypeStruct((positions, channels), F32)] * 2
    elements = positions * channels * states

    ends, span = pl.pallas_call(
        ends_kernel,
        grid=grid,
        in_specs=[wide, wide, state_wide],
        out_specs=[stacked, pl.BlockSpec((states, LANES), lambda c: (c, 0))],
        out_shape=[
            jax.ShapeDtypeStruct((2, columns * states, LANES), F32),
            jax.ShapeDtypeStruct((columns * states, LANES), F32),
        ],
        scratch_shapes=scratch,
        name="ends",
    )(signal, cotangent, decay_rate)

    rows = 2 * columns * states // devices
    sent = ends.reshape(devices, rows, LANES)
    gathered = lax.all_to_all(sent, "seq", 0, 0)

    weight = residue * jnp.sqrt(-jnp.expm1(-2.0 * decay_rate))
    y, z = pl.pallas_call(
        within_kernel,
        grid=grid,
        in_specs=[wide, wide, state_wide, state_wide, one_wide],
        out_specs=[wide, wide],
        out_shape=pair,
        scratch_shapes=scratch,
        cost_estimate=pl.CostEstimate(
            flops=12 * elements, bytes_accessed=12 * positions * channels, transcendentals=0
        ),
        name="within",
    )(signal, cotangent, decay_rate, weight, skip_gain.reshape(1, channels))

    share = lax.axis_index("seq").astype(jnp.int32).reshape(1)
    carried = pl.pallas_call(
        relay_kernel,
        in_specs=[
            pl.BlockSpec(memory_space=pltpu.SMEM),
            pl.BlockSpec(memory_space=pltpu.VMEM),
            pl.BlockSpec(memory_space=pltpu.VMEM),
        ],
        out_specs=pl.BlockSpec(memory_space=pltpu.VMEM),
        out_shape=jax.ShapeDtypeStruct((devices, rows, LANES), F32),
        name="relay",
    )(share, gathered, span)
    returned = lax.all_to_all(carried, "seq", 0, 0).reshape(2, columns * states, LANES)

    return pl.pallas_call(
        carry_kernel,
        grid=grid,
        in_specs=[wide, wide, state_wide, state_wide, stacked],
        out_specs=[wide, wide],
        out_shape=[jax.ShapeDtypeStruct(signal.shape, signal.dtype)] * 2,
        scratch_shapes=scratch,
        name="carry",
    )(y, z, decay_rate, weight, returned)


def solution(mesh):
    in_specs = (P("seq", "chan"), P("seq", "chan"), P(None, "chan"), P(None, "chan"), P("chan"))
    out_specs = (P("seq", "chan"), P("seq", "chan"))
    return jax.shard_map(
        lambda *arrays: tuple(shards(*arrays)),
        mesh=mesh,
        in_specs=in_specs,
        out_specs=out_specs,
        check_vma=False,
    )
```

time: 1300 us -> 74.3 us (0.06)
  the two profiles are of different devices: /device:TPU:6 before, /device:TPU:24 now
where the time goes in v1:
time: 74.3 us; the launch traced here: 73.5 us
  Pallas kernels  25.2 us (34%)
  starting transfers between devices  24.2 us (33%)
  waiting for transfers between devices  21.3 us (29%)
  local copies, waits for them, and re-layouts  1.31 us (2%)
    all_to_all x1, starting transfers between devices, shards(): gathered = lax.all_to_all(sent, 'seq', 0, 0)  18.6 us
    all_to_all x1, waiting for transfers between devices, shards(): gathered = lax.all_to_all(sent, 'seq', 0, 0)  16.3 us
    pallas_call x1, Pallas kernels, shards(): pl.pallas_call(within_kernel, grid=grid, in_specs=[wide, wide, state_wide...  10.4 us
    pallas_call x1, Pallas kernels, shards(): pl.pallas_call(carry_kernel, grid=grid, in_specs=[wide, wide, state_wide,...  6.73 us
    pallas_call x1, Pallas kernels, shards(): pl.pallas_call(ends_kernel, grid=grid, in_specs=[wide, wide, state_wide],...  6.41 us
    all_to_all x1, starting transfers between devices, shards(): lax.all_to_all(carried, 'seq', 0, 0).reshape(2, columns * states, LANES)  5.68 us
    all_to_all x1, waiting for transfers between devices, shards(): lax.all_to_all(carried, 'seq', 0, 0).reshape(2, columns * states, LANES)  4.99 us
    pallas_call x1, Pallas kernels, shards(): pl.pallas_call(relay_kernel, in_specs=[pl.BlockSpec(memory_space=pltpu.SM...  1.7 us
  transfers between devices with their start and end apart: 2, of which 2 were waited for; matrix products, arithmetic and copies ran while one was open for 1% of the time, Pallas kernels for 14%

profile of v1, /device:TPU:24, one launch (start us, length us, event | category | flops | bytes accessed | tf_op | source)
XLA Modules:
  0.0 73.5 jit_solution(14669314285120169811)
XLA Ops:
  0.6 6.4 %ends.1 = (f32[2,128,128]{2,1,0:T(8,128)}, f32[128,128]{1,0:T(8,128)}) custom-call(bf16[256,1024]{1,0:T(8,128)(2,1)} %signal_ref.3, bf16[256,1024]{1,0:T(8,128)(2,1)} %cotangent_ref.3, f32[16,1024]{1,0:T(8,128)} %rate_ref.5), custom_call_target="tpu_custom_call" | custom-call | tf_op jit(solution)/shard_map/ends/pallas_call | solution.py:176
  7.0 18.6 %all-to-all-start = ((f32[64,4,128]{2,1,0:T(4,128)}), f32[64,4,128]{2,1,0:T(4,128)S(1)}, u32[]{:S(2)}, u32[]{:S(2)}) async-start(f32[64,4,128]{2,1,0:T(4,128)} %bitcast.5), calls=%async_computation | async-start | bytes 262144 | tf_op jit(solution)/shard_map/all_to_all | solution.py:191
  25.6 16.3 %all-to-all-done.ends_ref = f32[64,4,128]{2,1,0:T(4,128)S(1)} async-done(((f32[64,4,128]{2,1,0:T(4,128)}), f32[64,4,128]{2,1,0:T(4,128)S(1)}, u32[]{:S(2)}, u32[]{:S(2)}) %all-to-all-start) | async-done | bytes 131104 | tf_op jit(solution)/shard_map/all_to_all | solution.py:191
  42.0 0.0 copy-start.1
  42.0 0.7 copy-done.1
  42.6 1.7 %relay.1 = f32[64,4,128]{2,1,0:T(4,128)} custom-call(s32[1]{0:T(128)} %bitcast.1.share_ref, f32[64,4,128]{2,1,0:T(4,128)} %copy-done.1, f32[128,128]{1,0:T(8,128)} %get-tuple-element.9.span_ref), custom_call_target="tpu_custom_call" | custom-call | tf_op jit(solution)/shard_map/relay/pallas_call | solution.py:208
  44.3 0.0 copy-start
  44.3 0.0 copy-start.3
  44.3 5.7 %all-to-all-start.1 = ((f32[64,4,128]{2,1,0:T(4,128)}), f32[64,4,128]{2,1,0:T(4,128)S(1)}, u32[]{:S(2)}, u32[]{:S(2)}) async-start(f32[64,4,128]{2,1,0:T(4,128)} %relay.1), calls=%async_computation.1 | async-start | bytes 262144 | tf_op jit(solution)/shard_map/all_to_all | solution.py:219
  50.0 0.0 copy-done
  50.0 0.0 copy-done.3
  50.0 0.7 sqrt_multiply_fusion.weight_ref
  50.7 10.4 %within.1 = (f32[256,1024]{1,0:T(8,128)}, f32[256,1024]{1,0:T(8,128)}) custom-call(bf16[256,1024]{1,0:T(8,128)(2,1)} %signal_ref.3, bf16[256,1024]{1,0:T(8,128)(2,1)} %cotangent_ref.3, f32[16,1024]{1,0:T(8,128)} %rate_ref.5, f32[16,1024]{1,0:T(8,128)} %sqrt_multiply_fusion.weight_ref, f32[1,1024]{1,0:T(1,128)} %bitcast.6), custom_call_target="tpu_custom_call" | custom-call | flops 50331648 | bytes 3145728 | tf_op jit(solution)/shard_map/within/pallas_call | solution.py:194
  61.1 5.0 %all-to-all-done.1 = f32[64,4,128]{2,1,0:T(4,128)S(1)} async-done(((f32[64,4,128]{2,1,0:T(4,128)}), f32[64,4,128]{2,1,0:T(4,128)S(1)}, u32[]{:S(2)}, u32[]{:S(2)}) %all-to-all-start.1) | async-done | bytes 131104 | tf_op jit(solution)/shard_map/all_to_all | solution.py:219
  66.1 0.0 copy-start.2
  66.1 0.7 copy-done.2
  66.8 6.7 %carry.1 = (bf16[256,1024]{1,0:T(8,128)(2,1)}, bf16[256,1024]{1,0:T(8,128)(2,1)}) custom-call(f32[256,1024]{1,0:T(8,128)} %get-tuple-element.6.y_ref, f32[256,1024]{1,0:T(8,128)} %get-tuple-element.7.z_ref, f32[16,1024]{1,0:T(8,128)} %rate_ref.5, f32[16,1024]{1,0:T(8,128)} %sqrt_multiply_fusion.weight_ref, f32[2,128,128]{2,1,0:T(8,128)} %bitcast.4), custom_call_target="tpu_custom_call" | custom-call | tf_op jit(solution)/shard_map/carry/pallas_call | solution.py:221
Async XLA Ops:
  7.0 34.9 %all-to-all-start = ((f32[64,4,128]{2,1,0:T(4,128)}), f32[64,4,128]{2,1,0:T(4,128)S(1)}, u32[]{:S(2)}, u32[]{:S(2)}) async-start(f32[64,4,128]{2,1,0:T(4,128)} %bitcast.5), calls=%async_computation | async-start | bytes 262144 | tf_op jit(solution)/shard_map/all_to_all | solution.py:191
  42.0 0.7 copy-start.1
  44.3 5.7 %copy-start = (f32[16,1024]{1,0:T(8,128)S(1)}, f32[16,1024]{1,0:T(8,128)}, u32[]{:S(2)}) copy-start(f32[16,1024]{1,0:T(8,128)} %rate_ref.5) | copy-start | bytes 196612
  44.3 5.7 %copy-start.3 = (f32[16,1024]{1,0:T(8,128)S(1)}, f32[16,1024]{1,0:T(8,128)}, u32[]{:S(2)}) copy-start(f32[16,1024]{1,0:T(8,128)} %param.8) | copy-start | bytes 196612
  44.3 21.8 %all-to-all-start.1 = ((f32[64,4,128]{2,1,0:T(4,128)}), f32[64,4,128]{2,1,0:T(4,128)S(1)}, u32[]{:S(2)}, u32[]{:S(2)}) async-start(f32[64,4,128]{2,1,0:T(4,128)} %relay.1), calls=%async_computation.1 | async-start | bytes 262144 | tf_op jit(solution)/shard_map/all_to_all | solution.py:219
  66.1 0.7 copy-start.2

commit v2 on v1

v2 whole, which is shorter than its diff:
```python
import functools
import jax
import jax.numpy as jnp
from jax import lax
from jax.experimental import pallas as pl
from jax.experimental.pallas import tpu as pltpu
from jax.sharding import PartitionSpec as P

SUB = 8
LANES = 128
F32 = jnp.float32


def row_of(table, n):
    return jnp.broadcast_to(table[n : n + 1, :], (SUB, LANES))


def block_index():
    return lax.broadcasted_iota(jnp.int32, (SUB, LANES), 0)


def blocked_position(x_ref, r, length):
    return x_ref[pl.ds(r, SUB, stride=length), :]


def block_ends(x_ref, decay, order, length):
    ends = [None] * len(decay)
    for step, r in enumerate(order):
        x = blocked_position(x_ref, r, length)
        for n in range(len(decay)):
            ends[n] = x if step == 0 else decay[n] * ends[n] + x
    return ends


def orders(length):
    return list(range(length)), list(range(length - 1, -1, -1))


def summed_positions(parts):
    at = block_index()
    low = at < 4
    parts = [
        jnp.where(low, parts[i], parts[i + 4])
        + pltpu.roll(jnp.where(low, parts[i + 4], parts[i]), 4, 0)
        for i in range(4)
    ]
    for by in (2, 1):
        low = lax.rem(at, 2 * by) < by
        parts = [
            jnp.where(
                low,
                parts[i] + pltpu.roll(parts[i], SUB - by, 0),
                parts[i + by] + pltpu.roll(parts[i + by], by, 0),
            )
            for i in range(by)
        ]
    return parts[0]


def ends_kernel(
    signal_hbm,
    cotangent_hbm,
    rate_hbm,
    ends_ref,
    signal_ref,
    cotangent_ref,
    rate_ref,
    sems,
    rate_sem,
):
    positions, width = signal_ref.shape
    states = rate_ref.shape[0]
    tiles = positions // SUB

    def part_copies(part):
        lanes = pl.ds(pl.multiple_of(part * 2 * LANES, 2 * LANES), 2 * LANES)
        return [
            pltpu.make_async_copy(hbm.at[:, lanes], ref.at[:, lanes], sems.at[side, part])
            for side, (hbm, ref) in enumerate(
                ((signal_hbm, signal_ref), (cotangent_hbm, cotangent_ref))
            )
        ]

    rate_copy = pltpu.make_async_copy(rate_hbm, rate_ref, rate_sem)
    rate_copy.start()
    for part in range(width // (2 * LANES)):
        for copy in part_copies(part):
            copy.start()
    rate_copy.wait()
    place = block_index()
    after = (SUB - 1 - place).astype(F32)
    before = place.astype(F32)

    def column(c, _):
        lanes = pl.ds(pl.multiple_of(c * LANES, LANES), LANES)
        rate = rate_ref[:, lanes]
        decay_table = jnp.exp(-rate * float(SUB))
        decay = [row_of(decay_table, n) for n in range(states)]
        ends = [None] * states
        starts = [None] * states
        for pair in range(tiles // 2):
            first = pair * 2 * SUB
            x = signal_ref[first : first + 2 * SUB, lanes].astype(F32)
            last = positions - 2 * SUB - first
            g = cotangent_ref[last : last + 2 * SUB, lanes].astype(F32)
            for half in range(2):
                xh = x[half * SUB : (half + 1) * SUB]
                gh = g[(1 - half) * SUB : (2 - half) * SUB]
                for n in range(states):
                    if pair == 0 and half == 0:
                        ends[n], starts[n] = xh, gh
                    else:
                        ends[n] = decay[n] * ends[n] + xh
                        starts[n] = decay[n] * starts[n] + gh
        for side, (sums, distance) in enumerate(((ends, after), (starts, before))):
            for low in range(0, states, SUB):
                parts = [
                    jnp.exp(-row_of(rate, n) * distance) * sums[n]
                    for n in range(low, low + SUB)
                ]
                at = pl.ds(pl.multiple_of(c * states + low, SUB), SUB)
                ends_ref[side, at, :] = summed_positions(parts)
        return 0

    def both_columns(part, _):
        for copy in part_copies(part):
            copy.wait()
        return lax.fori_loop(2 * part, 2 * part + 2, column, 0)

    lax.fori_loop(0, width // (2 * LANES), both_columns, 0)


def entering_states(ends, rate, length, forward):
    block = block_index()
    entering = []
    for n in range(len(ends)):
        total = ends[n]
        reach = 1
        while reach < SUB:
            ratio = jnp.exp(-row_of(rate, n) * float(length * reach))
            total = total + ratio * shifted_blocks(total, reach, block, forward)
            reach *= 2
        entering.append(shifted_blocks(total, 1, block, forward))
    return entering


def shifted_blocks(x, by, block, forward):
    if forward:
        return jnp.where(block >= by, pltpu.roll(x, by, 0), 0.0)
    return jnp.where(block < SUB - by, pltpu.roll(x, SUB - by, 0), 0.0)


def within_kernel(
    is_forward,
    x_hbm,
    rate_hbm,
    weight_hbm,
    gain_hbm,
    *refs,
):
    (
        both_ref,
        span_ref,
        whole_ref,
        x_ref,
        y_ref,
        rate_ref,
        weight_ref,
        gain_ref,
        sems,
        table_sems,
    ) = refs[-10:]
    local_ref = both_ref.at[0 if is_forward else 1]
    positions, width = whole_ref.shape
    length = positions // SUB
    states = rate_ref.shape[0]
    order = orders(length)[0 if is_forward else 1]
    place = block_index()
    distance = (place + 1 if is_forward else SUB - place).astype(F32)

    def part_copy(part):
        lanes = pl.ds(pl.multiple_of(part * 2 * LANES, 2 * LANES), 2 * LANES)
        return pltpu.make_async_copy(x_hbm.at[:, lanes], whole_ref.at[:, lanes], sems.at[part])

    table_copies = [
        pltpu.make_async_copy(hbm, ref, table_sems.at[i])
        for i, (hbm, ref) in enumerate(
            ((rate_hbm, rate_ref), (weight_hbm, weight_ref), (gain_hbm, gain_ref))
        )
    ]
    for copy in table_copies:
        copy.start()
    for part in range(width // (2 * LANES)):
        part_copy(part).start()
    for copy in table_copies:
        copy.wait()

    def column(c, _):
        lanes = pl.ds(pl.multiple_of(c * LANES, LANES), LANES)
        x_ref[...] = whole_ref[:, lanes].astype(F32)
        rate = rate_ref[:, lanes]
        rows = pl.ds(pl.multiple_of(c * states, states), states)
        span_ref[rows, :] = jnp.exp(-rate * float(positions))
        decay_table = jnp.exp(-rate)
        decay = [row_of(decay_table, n) for n in range(states)]
        weight_table = weight_ref[:, lanes]
        weight = [row_of(weight_table, n) for n in range(states)]
        gain = jnp.broadcast_to(gain_ref[:, lanes], (SUB, LANES))
        for n in range(states):
            reach = jnp.exp(-row_of(rate, n) * distance)
            local_ref[pl.ds(positions + n * SUB, SUB), lanes] = weight[n] * reach
        ends = block_ends(x_ref, decay, order, length)
        state = entering_states(ends, rate, length, is_forward)
        for r in order:
            x = blocked_position(x_ref, r, length)
            terms = [gain * x]
            for n in range(states):
                state[n] = decay[n] * state[n] + x
                terms.append(weight[n] * state[n])
            y_ref[pl.ds(r, SUB, stride=length), :] = added(terms)
        local_ref[pl.ds(0, positions), lanes] = y_ref[...]
        return 0

    def both_columns(part, _):
        part_copy(part).wait()
        return lax.fori_loop(2 * part, 2 * part + 2, column, 0)

    lax.fori_loop(0, width // (2 * LANES), both_columns, 0)


def added(terms):
    while len(terms) > 1:
        terms = [
            terms[i] + terms[i + 1] if i + 1 < len(terms) else terms[i]
            for i in range(0, len(terms), 2)
        ]
    return terms[0]


def relay_kernel(share_ref, ends_ref, span_ref, carried_ref):
    devices, rows, _ = ends_ref.shape
    share = share_ref[0]
    forward = share < devices // 2
    span = span_ref[pl.ds(lax.rem(share, devices // 2) * rows, rows), :]
    state = jnp.zeros(span.shape, F32)
    for step in range(devices):
        at = jnp.where(forward, step, devices - 1 - step)
        end = ends_ref[at]
        carried_ref[at] = state
        state = span * state + end


def carry_kernel(
    both_ref, rate_ref, carried_ref, out_hbm, grad_hbm, out_ref, grad_ref, sems
):
    positions, width = out_ref.shape
    states = rate_ref.shape[0]
    tiles = positions // SUB

    def part_copies(part):
        lanes = pl.ds(pl.multiple_of(part * 2 * LANES, 2 * LANES), 2 * LANES)
        return [
            pltpu.make_async_copy(ref.at[:, lanes], hbm.at[:, lanes], sems.at[side, part])
            for side, (hbm, ref) in enumerate(((out_hbm, out_ref), (grad_hbm, grad_ref)))
        ]

    def column(c, _):
        lanes = pl.ds(pl.multiple_of(c * LANES, LANES), LANES)
        decay_table = jnp.exp(-rate_ref[:, lanes] * float(SUB))
        decay = [row_of(decay_table, n) for n in range(states)]
        rows = pl.ds(pl.multiple_of(c * states, states), states)
        for side, result in enumerate((out_ref, grad_ref)):
            local_ref = both_ref.at[side]
            carried = carried_ref[side, rows, :]
            terms = [
                local_ref[pl.ds(positions + n * SUB, SUB), lanes] * row_of(carried, n)
                for n in range(states)
            ]
            for pair in range(tiles // 2):
                halves = []
                first = pair * 2 * SUB if side == 0 else positions - (pair + 1) * 2 * SUB
                for half in range(2):
                    if pair or half:
                        terms = [decay[n] * terms[n] for n in range(states)]
                    start = first + (half if side == 0 else 1 - half) * SUB
                    local = local_ref[pl.ds(start, SUB), lanes]
                    halves.append(added(terms) + local)
                if side:
                    halves.reverse()
                both = jnp.concatenate(halves, axis=0)
                result[first : first + 2 * SUB, lanes] = both.astype(result.dtype)
        return 0

    def both_columns(part, _):
        lax.fori_loop(2 * part, 2 * part + 2, column, 0)
        for copy in part_copies(part):
            copy.start()
        return 0

    lax.fori_loop(0, width // (2 * LANES), both_columns, 0)
    for part in range(width // (2 * LANES)):
        for copy in part_copies(part):
            copy.wait()


def vmem(mib):
    return pltpu.CompilerParams(vmem_limit_bytes=mib << 20)


def shards(signal, cotangent, decay_rate, residue, skip_gain):
    positions, channels = signal.shape
    states = decay_rate.shape[0]
    columns = channels // LANES
    devices = lax.axis_size("seq")
    anywhere = pl.BlockSpec(memory_space=pl.ANY)
    in_hbm = pl.BlockSpec(memory_space=pltpu.HBM)
    in_vmem = pl.BlockSpec(memory_space=pltpu.VMEM)
    elements = positions * channels * states
    whole = pltpu.VMEM((positions, channels), signal.dtype)
    column = pltpu.VMEM((positions, LANES), F32)
    table = pltpu.VMEM(decay_rate.shape, F32)
    copy_sems = pltpu.SemaphoreType.DMA((2, columns // 2))

    ends = pl.pallas_call(
        ends_kernel,
        in_specs=[in_hbm] * 3,
        out_specs=in_vmem,
        out_shape=jax.ShapeDtypeStruct((2, columns * states, LANES), F32),
        scratch_shapes=[
            whole,
            whole,
            table,
            copy_sems,
            pltpu.SemaphoreType.DMA,
        ],
        compiler_params=vmem(56),
        name="ends",
    )(signal, cotangent, decay_rate)

    rows = 2 * columns * states // devices
    sent = ends.reshape(devices, rows, LANES)
    gathered = lax.all_to_all(sent, "seq", 0, 0)

    weight = residue * jnp.sqrt(-jnp.expm1(-2.0 * decay_rate))
    gain = skip_gain.reshape(1, channels)
    depth = positions + states * SUB

    def within(is_forward, x, *other):
        return pl.pallas_call(
            functools.partial(within_kernel, is_forward),
            in_specs=[in_hbm] * 4 + [in_vmem] * len(other),
            out_specs=[in_vmem] * 2,
            out_shape=[
                jax.ShapeDtypeStruct((2, depth, channels), F32),
                jax.ShapeDtypeStruct((columns * states, LANES), F32),
            ],
            input_output_aliases={4: 0} if other else {},
            scratch_shapes=[
                whole,
                column,
                column,
                table,
                table,
                pltpu.VMEM((1, channels), F32),
                pltpu.SemaphoreType.DMA((columns // 2,)),
                pltpu.SemaphoreType.DMA((3,)),
            ],
            cost_estimate=pl.CostEstimate(
                flops=6 * elements, bytes_accessed=6 * positions * channels, transcendentals=0
            ),
            compiler_params=vmem(8),
            name="within_forward" if is_forward else "within_backward",
        )(x, decay_rate, weight, gain, *other)

    half, span = within(True, signal)
    both, _ = within(False, cotangent, half)
    share = lax.axis_index("seq").astype(jnp.int32).reshape(1)
    carried = pl.pallas_call(
        relay_kernel,
        in_specs=[pl.BlockSpec(memory_space=pltpu.SMEM), in_vmem, in_vmem],
        out_specs=in_vmem,
        out_shape=jax.ShapeDtypeStruct((devices, rows, LANES), F32),
        compiler_params=vmem(4),
        name="relay",
    )(share, gathered, span)
    returned = lax.all_to_all(carried, "seq", 0, 0).reshape(2, columns * states, LANES)

    return pl.pallas_call(
        carry_kernel,
        in_specs=[in_vmem] * 3,
        out_specs=[in_hbm] * 2,
        out_shape=[jax.ShapeDtypeStruct(signal.shape, signal.dtype)] * 2,
        scratch_shapes=[whole, whole, copy_sems],
        compiler_params=vmem(8),
        name="carry",
    )(both, decay_rate, returned)


def solution(mesh):
    in_specs = (P("seq", "chan"), P("seq", "chan"), P(None, "chan"), P(None, "chan"), P("chan"))
    out_specs = (P("seq", "chan"), P("seq", "chan"))
    return jax.shard_map(
        lambda *arrays: tuple(shards(*arrays)),
        mesh=mesh,
        in_specs=in_specs,
        out_specs=out_specs,
        check_vma=False,
    )
```

time: 74.3 us -> 68.2 us (0.918)
  waiting for transfers between devices: 21.3 us -> 15.1 us
  Pallas kernels: 25.2 us -> 19.7 us
  local copies, waits for them, and re-layouts: 1.31 us -> 5.13 us
  starting transfers between devices: 24.2 us -> 26.1 us
    all_to_all x1, waiting for transfers between devices: 16.3 us -> 7.63 us  [shards(): gathered = lax.all_to_all(sent, 'seq', 0, 0)]
    pallas_call x3 -> x4, Pallas kernels: 23.5 us -> 18.9 us  [the longest x2 11.1 us: within(): pl.pallas_call(functools.partial(within_kernel, is_forward), in_specs=[in...]
    unnamed x8 -> x14, local copies, waits for them, and re-layouts: 1.31 us -> 5.13 us
    all_to_all x1, waiting for transfers between devices: 4.99 us -> 7.49 us  [shards(): lax.all_to_all(carried, 'seq', 0, 0).reshape(2, columns * states, LANES)]
    all_to_all x1, starting transfers between devices: 5.68 us -> 7.52 us  [shards(): lax.all_to_all(carried, 'seq', 0, 0).reshape(2, columns * states, LANES)]
    pallas_call x1, Pallas kernels: 1.7 us -> 0.79 us  [shards(): pl.pallas_call(relay_kernel, in_specs=[pl.BlockSpec(memory_space=pltpu.SM...]
  transfers between devices with their start and end apart: 2 -> 2, of which waited for: 2 -> 2; matrix products, arithmetic and copies ran while one was open for 1% -> 1% of each run, Pallas kernels for 14% -> 16%
where the time goes in v2:
time: 68.2 us; the launch traced here: 67.7 us
  starting transfers between devices  26.1 us (38%)
  Pallas kernels  19.7 us (29%)
  waiting for transfers between devices  15.1 us (22%)
  local copies, waits for them, and re-layouts  5.13 us (8%)
  other arithmetic  0.92 us (1%)
  between operations  0.71 us (1%)
    all_to_all x1, starting transfers between devices, shards(): gathered = lax.all_to_all(sent, 'seq', 0, 0)  18.6 us
    pallas_call x2, Pallas kernels, within(): pl.pallas_call(functools.partial(within_kernel, is_forward), in_specs=[in...  11.1 us
    all_to_all x1, waiting for transfers between devices, shards(): gathered = lax.all_to_all(sent, 'seq', 0, 0)  7.63 us
    all_to_all x1, starting transfers between devices, shards(): lax.all_to_all(carried, 'seq', 0, 0).reshape(2, columns * states, LANES)  7.52 us
    all_to_all x1, waiting for transfers between devices, shards(): lax.all_to_all(carried, 'seq', 0, 0).reshape(2, columns * states, LANES)  7.49 us
    unnamed x14, local copies, waits for them, and re-layouts  5.13 us
    pallas_call x1, Pallas kernels, shards(): pl.pallas_call(ends_kernel, in_specs=[in_hbm] * 3, out_specs=in_vmem, out...  4.68 us
    pallas_call x1, Pallas kernels, shards(): pl.pallas_call(carry_kernel, in_specs=[in_vmem] * 3, out_specs=[in_hbm] *...  3.18 us
  transfers between devices with their start and end apart: 2, of which 2 were waited for; matrix products, arithmetic and copies ran while one was open for 1% of the time, Pallas kernels for 16%

profile of v2, /device:TPU:24, one launch (start us, length us, event | category | flops | bytes accessed | tf_op | source)
XLA Modules:
  0.0 67.7 jit_solution(2819002640892150815)
XLA Ops:
  0.6 0.0 copy-start.4
  0.6 4.7 %ends.1 = f32[2,128,128]{2,1,0:T(8,128)} custom-call(bf16[256,1024]{1,0:T(8,128)(2,1)} %signal_hbm.1, bf16[256,1024]{1,0:T(8,128)(2,1)} %cotangent_hbm.1, f32[16,1024]{1,0:T(8,128)} %rate_ref.1), custom_call_target="tpu_custom_call" | custom-call | tf_op jit(solution)/shard_map/ends/pallas_call | solution.py:324
  5.3 18.6 %all-to-all-start = ((f32[64,4,128]{2,1,0:T(4,128)}), f32[64,4,128]{2,1,0:T(4,128)S(1)}, u32[]{:S(2)}, u32[]{:S(2)}) async-start(f32[64,4,128]{2,1,0:T(4,128)} %bitcast.7), calls=%async_computation | async-start | bytes 262144 | tf_op jit(solution)/shard_map/all_to_all | solution.py:342
  23.9 0.9 %sqrt_multiply_fusion.weight_hbm = f32[16,1024]{1,0:T(8,128)S(1)} fusion(f32[16,1024]{1,0:T(8,128)} %param.8, f32[16,1024]{1,0:T(8,128)} %rate_ref.1), kind=kLoop, calls=%fused_computation | loop fusion | flops 49152 | bytes 196608 | tf_op jit(solution)/shard_map/mul | solution.py:344
  24.8 0.0 copy-start
  24.8 1.0 %copy-done = bf16[256,1024]{1,0:T(8,128)(2,1)S(1)} copy-done((bf16[256,1024]{1,0:T(8,128)(2,1)S(1)}, bf16[256,1024]{1,0:T(8,128)(2,1)}, u32[]{:S(2)}) %copy-start) | copy-done | bytes 524312
  25.9 0.0 copy-start.2
  25.9 0.8 %copy-done.2 = f32[16,1024]{1,0:T(8,128)S(1)} copy-done((f32[16,1024]{1,0:T(8,128)S(1)}, f32[16,1024]{1,0:T(8,128)}, u32[]{:S(2)}) %copy-start.2) | copy-done | bytes 65560
  26.7 0.0 copy-start.5
  26.7 0.7 %copy-done.5 = f32[1024]{0:T(1024)S(1)} copy-done((f32[1024]{0:T(1024)S(1)}, f32[1024]{0:T(1024)}, u32[]{:S(2)}) %copy-start.5) | copy-done | bytes 4120
  27.4 5.2 %within_forward.1 = (f32[2,384,1024]{2,1,0:T(8,128)S(1)}, f32[128,128]{1,0:T(8,128)S(1)}) custom-call(bf16[256,1024]{1,0:T(8,128)(2,1)S(1)} %copy-done, f32[16,1024]{1,0:T(8,128)S(1)} %copy-done.2, f32[16,1024]{1,0:T(8,128)S(1)} %sqrt_multiply_fusion.weight_hbm, f32[1,1024]{1,0:T(1,128)S(1)} %bitcast.5), custom_call_target="tpu_custom_call" | custom-call | flops 25165824 | bytes 1572864 | tf_op jit(solution)/shard_map/within_forward/pallas_call | solution.py:349
  32.6 7.6 %all-to-all-done.ends_ref = f32[64,4,128]{2,1,0:T(4,128)S(1)} async-done(((f32[64,4,128]{2,1,0:T(4,128)}), f32[64,4,128]{2,1,0:T(4,128)S(1)}, u32[]{:S(2)}, u32[]{:S(2)}) %all-to-all-start) | async-done | bytes 131104 | tf_op jit(solution)/shard_map/all_to_all | solution.py:342
  40.3 0.8 %relay.1 = f32[64,4,128]{2,1,0:T(4,128)} custom-call(s32[1]{0:T(128)} %bitcast.1.share_ref, f32[64,4,128]{2,1,0:T(4,128)S(1)} %all-to-all-done.ends_ref, f32[128,128]{1,0:T(8,128)S(1)} %get-tuple-element.7.span_ref), custom_call_target="tpu_custom_call" | custom-call | tf_op jit(solution)/shard_map/relay/pallas_call | solution.py:378
  41.0 7.5 %all-to-all-start.1 = ((f32[64,4,128]{2,1,0:T(4,128)}), f32[64,4,128]{2,1,0:T(4,128)S(1)}, u32[]{:S(2)}, u32[]{:S(2)}) async-start(f32[64,4,128]{2,1,0:T(4,128)} %relay.1), calls=%async_computation.1 | async-start | bytes 262144 | tf_op jit(solution)/shard_map/all_to_all | solution.py:386
  48.6 0.0 copy-start.1
  48.6 1.0 %copy-done.1 = bf16[256,1024]{1,0:T(8,128)(2,1)S(1)} copy-done((bf16[256,1024]{1,0:T(8,128)(2,1)S(1)}, bf16[256,1024]{1,0:T(8,128)(2,1)}, u32[]{:S(2)}) %copy-start.1) | copy-done | bytes 524312
  49.6 0.0 copy-start.3
  49.6 0.8 %copy-done.3 = f32[16,1024]{1,0:T(8,128)S(1)} copy-done((f32[16,1024]{1,0:T(8,128)S(1)}, f32[16,1024]{1,0:T(8,128)}, u32[]{:S(2)}) %copy-start.3) | copy-done | bytes 65560
  50.5 0.0 copy-start.6
  50.5 0.7 %copy-done.6 = f32[1024]{0:T(1024)S(1)} copy-done((f32[1024]{0:T(1024)S(1)}, f32[1024]{0:T(1024)}, u32[]{:S(2)}) %copy-start.6) | copy-done | bytes 4120
  51.2 5.8 %within_backward.1 = (f32[2,384,1024]{2,1,0:T(8,128)S(1)}, f32[128,128]{1,0:T(8,128)}) custom-call(bf16[256,1024]{1,0:T(8,128)(2,1)S(1)} %copy-done.1, f32[16,1024]{1,0:T(8,128)S(1)} %copy-done.3, f32[16,1024]{1,0:T(8,128)S(1)} %sqrt_multiply_fusion.weight_hbm, f32[1,1024]{1,0:T(1,128)S(1)} %bitcast.6, ...), custom_call_target="tpu_custom_call", output_to_operand_aliasing={{0}: (4, {})} | custom-call | flops 25165824 | bytes 1572864 | tf_op jit(solution)/shard_map/within_backward/pallas_call | solution.py:349
  57.0 7.5 %all-to-all-done.1 = f32[64,4,128]{2,1,0:T(4,128)S(1)} async-done(((f32[64,4,128]{2,1,0:T(4,128)}), f32[64,4,128]{2,1,0:T(4,128)S(1)}, u32[]{:S(2)}, u32[]{:S(2)}) %all-to-all-start.1) | async-done | bytes 131104 | tf_op jit(solution)/shard_map/all_to_all | solution.py:386
  64.5 0.0 copy-done.4
  64.5 3.2 %carry.1 = (bf16[256,1024]{1,0:T(8,128)(2,1)}, bf16[256,1024]{1,0:T(8,128)(2,1)}) custom-call(f32[2,384,1024]{2,1,0:T(8,128)S(1)} %get-tuple-element.6.both_ref, f32[16,1024]{1,0:T(8,128)S(1)} %copy-done.4, f32[2,128,128]{2,1,0:T(8,128)S(1)} %bitcast.4), custom_call_target="tpu_custom_call" | custom-call | tf_op jit(solution)/shard_map/carry/pallas_call | solution.py:388
Async XLA Ops:
  0.6 63.9 %copy-start.4 = (f32[16,1024]{1,0:T(8,128)S(1)}, f32[16,1024]{1,0:T(8,128)}, u32[]{:S(2)}) copy-start(f32[16,1024]{1,0:T(8,128)} %rate_ref.1) | copy-start | bytes 196612
  5.3 34.9 %all-to-all-start = ((f32[64,4,128]{2,1,0:T(4,128)}), f32[64,4,128]{2,1,0:T(4,128)S(1)}, u32[]{:S(2)}, u32[]{:S(2)}) async-start(f32[64,4,128]{2,1,0:T(4,128)} %bitcast.7), calls=%async_computation | async-start | bytes 262144 | tf_op jit(solution)/shard_map/all_to_all | solution.py:342
  24.8 1.0 %copy-start = (bf16[256,1024]{1,0:T(8,128)(2,1)S(1)}, bf16[256,1024]{1,0:T(8,128)(2,1)}, u32[]{:S(2)}) copy-start(bf16[256,1024]{1,0:T(8,128)(2,1)} %signal_hbm.1) | copy-start | bytes 1572868
  25.9 0.8 %copy-start.2 = (f32[16,1024]{1,0:T(8,128)S(1)}, f32[16,1024]{1,0:T(8,128)}, u32[]{:S(2)}) copy-start(f32[16,1024]{1,0:T(8,128)} %rate_ref.1) | copy-start | bytes 196612
  26.7 0.7 %copy-start.5 = (f32[1024]{0:T(1024)S(1)}, f32[1024]{0:T(1024)}, u32[]{:S(2)}) copy-start(f32[1024]{0:T(1024)} %param.9) | copy-start | bytes 12292
  41.0 23.4 %all-to-all-start.1 = ((f32[64,4,128]{2,1,0:T(4,128)}), f32[64,4,128]{2,1,0:T(4,128)S(1)}, u32[]{:S(2)}, u32[]{:S(2)}) async-start(f32[64,4,128]{2,1,0:T(4,128)} %relay.1), calls=%async_computation.1 | async-start | bytes 262144 | tf_op jit(solution)/shard_map/all_to_all | solution.py:386
  48.6 1.0 %copy-start.1 = (bf16[256,1024]{1,0:T(8,128)(2,1)S(1)}, bf16[256,1024]{1,0:T(8,128)(2,1)}, u32[]{:S(2)}) copy-start(bf16[256,1024]{1,0:T(8,128)(2,1)} %cotangent_hbm.1) | copy-start | bytes 1572868
  49.6 0.8 %copy-start.3 = (f32[16,1024]{1,0:T(8,128)S(1)}, f32[16,1024]{1,0:T(8,128)}, u32[]{:S(2)}) copy-start(f32[16,1024]{1,0:T(8,128)} %rate_ref.1) | copy-start | bytes 196612
  50.5 0.7 %copy-start.6 = (f32[1024]{0:T(1024)S(1)}, f32[1024]{0:T(1024)}, u32[]{:S(2)}) copy-start(f32[1024]{0:T(1024)} %param.9) | copy-start | bytes 12292

commit v3 on v2

--- a/solution.py
+++ b/solution.py
@@ -160,7 +160,6 @@
 ):
     (
         both_ref,
-        span_ref,
         whole_ref,
         x_ref,
         y_ref,
@@ -169,7 +168,7 @@
         gain_ref,
         sems,
         table_sems,
-    ) = refs[-10:]
+    ) = refs[-9:]
     local_ref = both_ref.at[0 if is_forward else 1]
     positions, width = whole_ref.shape
     length = positions // SUB
@@ -199,8 +198,6 @@
         lanes = pl.ds(pl.multiple_of(c * LANES, LANES), LANES)
         x_ref[...] = whole_ref[:, lanes].astype(F32)
         rate = rate_ref[:, lanes]
-        rows = pl.ds(pl.multiple_of(c * states, states), states)
-        span_ref[rows, :] = jnp.exp(-rate * float(positions))
         decay_table = jnp.exp(-rate)
         decay = [row_of(decay_table, n) for n in range(states)]
         weight_table = weight_ref[:, lanes]
@@ -349,11 +346,8 @@
         return pl.pallas_call(
             functools.partial(within_kernel, is_forward),
             in_specs=[in_hbm] * 4 + [in_vmem] * len(other),
-            out_specs=[in_vmem] * 2,
-            out_shape=[
-                jax.ShapeDtypeStruct((2, depth, channels), F32),
-                jax.ShapeDtypeStruct((columns * states, LANES), F32),
-            ],
+            out_specs=in_vmem,
+            out_shape=jax.ShapeDtypeStruct((2, depth, channels), F32),
             input_output_aliases={4: 0} if other else {},
             scratch_shapes=[
                 whole,
@@ -372,8 +366,10 @@
             name="within_forward" if is_forward else "within_backward",
         )(x, decay_rate, weight, gain, *other)
 
-    half, span = within(True, signal)
-    both, _ = within(False, cotangent, half)
+    rate_then, _ = lax.optimization_barrier((decay_rate, ends))
+    span = jnp.exp(-float(positions) * rate_then).reshape(states, columns, LANES)
+    span = span.swapaxes(0, 1).reshape(columns * states, LANES)
+
     share = lax.axis_index("seq").astype(jnp.int32).reshape(1)
     carried = pl.pallas_call(
         relay_kernel,
@@ -383,6 +379,8 @@
         compiler_params=vmem(4),
         name="relay",
     )(share, gathered, span)
+    signal, cotangent, _ = lax.optimization_barrier((signal, cotangent, carried))
+    both = within(False, cotangent, within(True, signal))
     returned = lax.all_to_all(carried, "seq", 0, 0).reshape(2, columns * states, LANES)
 
     return pl.pallas_call(

time: 68.2 us -> 66.3 us (0.972)
  local copies, waits for them, and re-layouts: 5.13 us -> 2.58 us
  waiting for transfers between devices: 15.1 us -> 17.6 us
  starting transfers between devices: 26.1 us -> 24.1 us
  other arithmetic: 0.92 us -> 1.78 us
    all_to_all x1, waiting for transfers between devices: 7.63 us -> 15.5 us  [shards(): gathered = lax.all_to_all(sent, 'seq', 0, 0)]
    all_to_all x1, waiting for transfers between devices: 7.49 us -> 2.08 us  [shards(): lax.all_to_all(carried, 'seq', 0, 0).reshape(2, columns * states, LANES)]
    unnamed x14 -> x12, local copies, waits for them, and re-layouts: 5.13 us -> 2.58 us
    all_to_all x1, starting transfers between devices: 7.52 us -> 5.55 us  [shards(): lax.all_to_all(carried, 'seq', 0, 0).reshape(2, columns * states, LANES)]
    reshape x0 -> x1, other arithmetic: none -> 0.86 us  [shards(): jnp.exp(-float(positions) * rate_then).reshape(states, columns, LANES)]
  transfers between devices with their start and end apart: 2 -> 2, of which waited for: 2 -> 2; matrix products, arithmetic and copies ran while one was open for 1% -> 3% of each run, Pallas kernels for 16% -> 16%
where the time goes in v3:
time: 66.3 us; the launch traced here: 65.9 us
  starting transfers between devices  24.1 us (36%)
  Pallas kernels  19.1 us (29%)
  waiting for transfers between devices  17.6 us (27%)
  local copies, waits for them, and re-layouts  2.58 us (4%)
  other arithmetic  1.78 us (3%)
  between operations  0.72 us (1%)
    all_to_all x1, starting transfers between devices, shards(): gathered = lax.all_to_all(sent, 'seq', 0, 0)  18.6 us
    all_to_all x1, waiting for transfers between devices, shards(): gathered = lax.all_to_all(sent, 'seq', 0, 0)  15.5 us
    pallas_call x2, Pallas kernels, within(): pl.pallas_call(functools.partial(within_kernel, is_forward), in_specs=[in...  10.5 us
    all_to_all x1, starting transfers between devices, shards(): lax.all_to_all(carried, 'seq', 0, 0).reshape(2, columns * states, LANES)  5.55 us
    pallas_call x1, Pallas kernels, shards(): pl.pallas_call(ends_kernel, in_specs=[in_hbm] * 3, out_specs=in_vmem, out...  4.65 us
    pallas_call x1, Pallas kernels, shards(): pl.pallas_call(carry_kernel, in_specs=[in_vmem] * 3, out_specs=[in_hbm] *...  3.18 us
    unnamed x12, local copies, waits for them, and re-layouts  2.58 us
    all_to_all x1, waiting for transfers between devices, shards(): lax.all_to_all(carried, 'seq', 0, 0).reshape(2, columns * states, LANES)  2.08 us
  transfers between devices with their start and end apart: 2, of which 2 were waited for; matrix products, arithmetic and copies ran while one was open for 3% of the time, Pallas kernels for 16%

profile of v3, /device:TPU:24, one launch (start us, length us, event | category | flops | bytes accessed | tf_op | source)
XLA Modules:
  0.0 65.9 jit_solution(8553342607368602067)
XLA Ops:
  0.6 0.0 copy-start.5
  0.6 4.7 %ends.1 = f32[2,128,128]{2,1,0:T(8,128)} custom-call(bf16[256,1024]{1,0:T(8,128)(2,1)} %x_hbm, bf16[256,1024]{1,0:T(8,128)(2,1)} %x_hbm.1, f32[16,1024]{1,0:T(8,128)} %rate_ref.1), custom_call_target="tpu_custom_call" | custom-call | tf_op jit(solution)/shard_map/ends/pallas_call | solution.py:321
  5.3 18.6 %all-to-all-start = ((f32[64,4,128]{2,1,0:T(4,128)}), f32[64,4,128]{2,1,0:T(4,128)S(1)}, u32[]{:S(2)}, u32[]{:S(2)}) async-start(f32[64,4,128]{2,1,0:T(4,128)} %bitcast.16), calls=%async_computation | async-start | bytes 262144 | tf_op jit(solution)/shard_map/all_to_all | solution.py:339
  23.9 0.9 %copy_bitcast_fusion = f32[16,8,128]{2,0,1:T(8,128)S(1)} fusion(f32[16,1024]{1,0:T(8,128)} %rate_ref.1), kind=kLoop, calls=%fused_computation | loop fusion | flops 16384 | bytes 131072 | tf_op jit(solution)/shard_map/reshape | solution.py:370
  24.7 15.5 %all-to-all-done.ends_ref = f32[64,4,128]{2,1,0:T(4,128)S(1)} async-done(((f32[64,4,128]{2,1,0:T(4,128)}), f32[64,4,128]{2,1,0:T(4,128)S(1)}, u32[]{:S(2)}, u32[]{:S(2)}) %all-to-all-start) | async-done | bytes 131104 | tf_op jit(solution)/shard_map/all_to_all | solution.py:339
  40.2 0.8 %relay.1 = f32[64,4,128]{2,1,0:T(4,128)} custom-call(s32[1]{0:T(128)} %bitcast.share_ref, f32[64,4,128]{2,1,0:T(4,128)S(1)} %all-to-all-done.ends_ref, f32[128,128]{1,0:T(8,128)S(1)} %bitcast.13), custom_call_target="tpu_custom_call" | custom-call | tf_op jit(solution)/shard_map/relay/pallas_call | solution.py:374
  41.0 5.6 %all-to-all-start.1 = ((f32[64,4,128]{2,1,0:T(4,128)}), f32[64,4,128]{2,1,0:T(4,128)S(1)}, u32[]{:S(2)}, u32[]{:S(2)}) async-start(f32[64,4,128]{2,1,0:T(4,128)} %relay.1), calls=%async_computation.1 | async-start | bytes 262144 | tf_op jit(solution)/shard_map/all_to_all | solution.py:384
  46.6 0.9 %sqrt_multiply_fusion.weight_hbm = f32[16,1024]{1,0:T(8,128)S(1)} fusion(f32[16,1024]{1,0:T(8,128)} %param.8, f32[16,1024]{1,0:T(8,128)} %rate_ref.1), kind=kLoop, calls=%fused_computation.1 | loop fusion | flops 49152 | bytes 196608 | tf_op jit(solution)/shard_map/mul | solution.py:341
  47.5 0.0 copy-start
  47.5 0.8 %copy-done = f32[16,1024]{1,0:T(8,128)S(1)} copy-done((f32[16,1024]{1,0:T(8,128)S(1)}, f32[16,1024]{1,0:T(8,128)}, u32[]{:S(2)}) %copy-start) | copy-done | bytes 65560
  48.3 0.0 copy-start.3
  48.4 1.0 %copy-done.3 = bf16[256,1024]{1,0:T(8,128)(2,1)S(1)} copy-done((bf16[256,1024]{1,0:T(8,128)(2,1)S(1)}, bf16[256,1024]{1,0:T(8,128)(2,1)}, u32[]{:S(2)}) %copy-start.3) | copy-done | bytes 524312
  49.4 0.0 copy-start.4
  49.4 0.7 %copy-done.4 = f32[1024]{0:T(1024)S(1)} copy-done((f32[1024]{0:T(1024)S(1)}, f32[1024]{0:T(1024)}, u32[]{:S(2)}) %copy-start.4) | copy-done | bytes 4120
  50.1 0.0 copy-start.2
  50.1 5.2 %within_forward.1.refs_0_ = f32[2,384,1024]{2,1,0:T(8,128)S(1)} custom-call(bf16[256,1024]{1,0:T(8,128)(2,1)S(1)} %copy-done.3, f32[16,1024]{1,0:T(8,128)S(1)} %copy-done, f32[16,1024]{1,0:T(8,128)S(1)} %sqrt_multiply_fusion.weight_hbm, f32[1,1024]{1,0:T(1,128)S(1)} %bitcast.14), custom_call_target="tpu_custom_call" | custom-call | flops 25165824 | bytes 1572864 | tf_op jit(solution)/shard_map/within_forward/pallas_call | solution.py:346
  55.3 0.0 copy-done.5
  55.3 0.0 copy-done.2
  55.3 0.0 copy-start.1
  55.4 5.2 %within_backward.1.both_ref = f32[2,384,1024]{2,1,0:T(8,128)S(1)} custom-call(bf16[256,1024]{1,0:T(8,128)(2,1)S(1)} %copy-done.2, f32[16,1024]{1,0:T(8,128)S(1)} %copy-done, f32[16,1024]{1,0:T(8,128)S(1)} %sqrt_multiply_fusion.weight_hbm, f32[1,1024]{1,0:T(1,128)S(1)} %bitcast.15, ...), custom_call_target="tpu_custom_call", output_to_operand_aliasing={{}: (4, {})} | custom-call | flops 25165824 | bytes 1572864 | tf_op jit(solution)/shard_map/within_backward/pallas_call | solution.py:346
  60.6 2.1 %all-to-all-done.1 = f32[64,4,128]{2,1,0:T(4,128)S(1)} async-done(((f32[64,4,128]{2,1,0:T(4,128)}), f32[64,4,128]{2,1,0:T(4,128)S(1)}, u32[]{:S(2)}, u32[]{:S(2)}) %all-to-all-start.1) | async-done | bytes 131104 | tf_op jit(solution)/shard_map/all_to_all | solution.py:384
  62.7 0.0 copy-done.1
  62.7 3.2 %carry.1 = (bf16[256,1024]{1,0:T(8,128)(2,1)}, bf16[256,1024]{1,0:T(8,128)(2,1)}) custom-call(f32[2,384,1024]{2,1,0:T(8,128)S(1)} %within_backward.1.both_ref, f32[16,1024]{1,0:T(8,128)S(1)} %copy-done.1, f32[2,128,128]{2,1,0:T(8,128)S(1)} %bitcast.12), custom_call_target="tpu_custom_call" | custom-call | tf_op jit(solution)/shard_map/carry/pallas_call | solution.py:386
Async XLA Ops:
  0.6 54.7 %copy-start.5 = (f32[1024]{0:T(1024)S(1)}, f32[1024]{0:T(1024)}, u32[]{:S(2)}) copy-start(f32[1024]{0:T(1024)} %param.9) | copy-start | bytes 12292
  5.3 34.9 %all-to-all-start = ((f32[64,4,128]{2,1,0:T(4,128)}), f32[64,4,128]{2,1,0:T(4,128)S(1)}, u32[]{:S(2)}, u32[]{:S(2)}) async-start(f32[64,4,128]{2,1,0:T(4,128)} %bitcast.16), calls=%async_computation | async-start | bytes 262144 | tf_op jit(solution)/shard_map/all_to_all | solution.py:339
  41.0 21.7 %all-to-all-start.1 = ((f32[64,4,128]{2,1,0:T(4,128)}), f32[64,4,128]{2,1,0:T(4,128)S(1)}, u32[]{:S(2)}, u32[]{:S(2)}) async-start(f32[64,4,128]{2,1,0:T(4,128)} %relay.1), calls=%async_computation.1 | async-start | bytes 262144 | tf_op jit(solution)/shard_map/all_to_all | solution.py:384
  47.5 0.8 %copy-start = (f32[16,1024]{1,0:T(8,128)S(1)}, f32[16,1024]{1,0:T(8,128)}, u32[]{:S(2)}) copy-start(f32[16,1024]{1,0:T(8,128)} %rate_ref.1) | copy-start | bytes 196612
  48.3 1.0 %copy-start.3 = (bf16[256,1024]{1,0:T(8,128)(2,1)S(1)}, bf16[256,1024]{1,0:T(8,128)(2,1)}, u32[]{:S(2)}) copy-start(bf16[256,1024]{1,0:T(8,128)(2,1)} %x_hbm) | copy-start | bytes 1572868
  49.4 0.7 %copy-start.4 = (f32[1024]{0:T(1024)S(1)}, f32[1024]{0:T(1024)}, u32[]{:S(2)}) copy-start(f32[1024]{0:T(1024)} %param.9) | copy-start | bytes 12292
  50.1 5.3 %copy-start.2 = (bf16[256,1024]{1,0:T(8,128)(2,1)S(1)}, bf16[256,1024]{1,0:T(8,128)(2,1)}, u32[]{:S(2)}) copy-start(bf16[256,1024]{1,0:T(8,128)(2,1)} %x_hbm.1) | copy-start | bytes 1572868
  55.3 7.3 %copy-start.1 = (f32[16,1024]{1,0:T(8,128)S(1)}, f32[16,1024]{1,0:T(8,128)}, u32[]{:S(2)}) copy-start(f32[16,1024]{1,0:T(8,128)} %rate_ref.1) | copy-start | bytes 196612

commit v4 on v3

--- a/solution.py
+++ b/solution.py
@@ -9,6 +9,7 @@
 SUB = 8
 LANES = 128
 F32 = jnp.float32
+ROOT, ROOT_OF = 41, 64
 
 
 def row_of(table, n):
@@ -234,14 +235,15 @@
     return terms[0]
 
 
-def relay_kernel(share_ref, ends_ref, span_ref, carried_ref):
+def relay_kernel(first, share_ref, ends_ref, span_ref, carried_ref):
     devices, rows, _ = ends_ref.shape
     share = share_ref[0]
     forward = share < devices // 2
     span = span_ref[pl.ds(lax.rem(share, devices // 2) * rows, rows), :]
     state = jnp.zeros(span.shape, F32)
     for step in range(devices):
-        at = jnp.where(forward, step, devices - 1 - step)
+        ahead, behind = (step - first) % devices, (devices - 1 - step - first) % devices
+        at = jnp.where(forward, ahead, behind)
         end = ends_ref[at]
         carried_ref[at] = state
         state = span * state + end
@@ -336,7 +338,16 @@
 
     rows = 2 * columns * states // devices
     sent = ends.reshape(devices, rows, LANES)
-    gathered = lax.all_to_all(sent, "seq", 0, 0)
+    first = ROOT * devices // ROOT_OF
+    group = [[(first + i) % devices for i in range(devices)]]
+    exchanged = functools.partial(
+        lax.all_to_all,
+        axis_name="seq",
+        split_axis=0,
+        concat_axis=0,
+        axis_index_groups=group,
+    )
+    gathered = exchanged(sent)
 
     weight = residue * jnp.sqrt(-jnp.expm1(-2.0 * decay_rate))
     gain = skip_gain.reshape(1, channels)
@@ -370,9 +381,10 @@
     span = jnp.exp(-float(positions) * rate_then).reshape(states, columns, LANES)
     span = span.swapaxes(0, 1).reshape(columns * states, LANES)
 
-    share = lax.axis_index("seq").astype(jnp.int32).reshape(1)
+    share = lax.rem(lax.axis_index("seq") + (devices - first), devices)
+    share = share.astype(jnp.int32).reshape(1)
     carried = pl.pallas_call(
-        relay_kernel,
+        functools.partial(relay_kernel, first),
         in_specs=[pl.BlockSpec(memory_space=pltpu.SMEM), in_vmem, in_vmem],
         out_specs=in_vmem,
         out_shape=jax.ShapeDtypeStruct((devices, rows, LANES), F32),
@@ -381,7 +393,7 @@
     )(share, gathered, span)
     signal, cotangent, _ = lax.optimization_barrier((signal, cotangent, carried))
     both = within(False, cotangent, within(True, signal))
-    returned = lax.all_to_all(carried, "seq", 0, 0).reshape(2, columns * states, LANES)
+    returned = exchanged(carried).reshape(2, columns * states, LANES)
 
     return pl.pallas_call(
         carry_kernel,

time: 66.3 us -> 67.2 us (1.014)
  starting transfers between devices: 24.1 us -> 36.5 us
  waiting for transfers between devices: 17.6 us -> 6.1 us
    all_to_all x2, starting transfers between devices: 24.1 us -> 36.5 us  [the longest x1 21.6 us: shards(): gathered = exchanged(sent)]
    all_to_all x2, waiting for transfers between devices: 17.6 us -> 6.1 us  [the longest x1 6.1 us: shards(): gathered = exchanged(sent)]
  transfers between devices with their start and end apart: 2 -> 2, of which waited for: 2 -> 1; matrix products, arithmetic and copies ran while one was open for 3% -> 3% of each run, Pallas kernels for 16% -> 16%
where the time goes in v4:
time: 67.2 us; the launch traced here: 66.8 us
  starting transfers between devices  36.5 us (54%)
  Pallas kernels  19.1 us (28%)
  waiting for transfers between devices  6.1 us (9%)
  local copies, waits for them, and re-layouts  2.58 us (4%)
  other arithmetic  1.78 us (3%)
  between operations  0.74 us (1%)
    all_to_all x1, starting transfers between devices, shards(): gathered = exchanged(sent)  21.6 us
    all_to_all x1, starting transfers between devices, shards(): returned = exchanged(carried).reshape(2, columns * states, LANES)  14.8 us
    pallas_call x2, Pallas kernels, within(): pl.pallas_call(functools.partial(within_kernel, is_forward), in_specs=[in...  10.5 us
    all_to_all x1, waiting for transfers between devices, shards(): gathered = exchanged(sent)  6.1 us
    pallas_call x1, Pallas kernels, shards(): pl.pallas_call(ends_kernel, in_specs=[in_hbm] * 3, out_specs=in_vmem, out...  4.65 us
    pallas_call x1, Pallas kernels, shards(): pl.pallas_call(carry_kernel, in_specs=[in_vmem] * 3, out_specs=[in_hbm] *...  3.18 us
    unnamed x12, local copies, waits for them, and re-layouts  2.58 us
  transfers between devices with their start and end apart: 2, of which 1 were waited for; matrix products, arithmetic and copies ran while one was open for 3% of the time, Pallas kernels for 16%

profile of v4, /device:TPU:24, one launch (start us, length us, event | category | flops | bytes accessed | tf_op | source)
XLA Modules:
  0.0 66.8 jit_solution(17096211773836529559)
XLA Ops:
  0.6 0.0 copy-start.5
  0.6 4.7 %ends.1 = f32[2,128,128]{2,1,0:T(8,128)} custom-call(bf16[256,1024]{1,0:T(8,128)(2,1)} %x_hbm, bf16[256,1024]{1,0:T(8,128)(2,1)} %x_hbm.1, f32[16,1024]{1,0:T(8,128)} %rate_ref.1), custom_call_target="tpu_custom_call" | custom-call | tf_op jit(solution)/shard_map/ends/pallas_call | solution.py:323
  5.3 21.6 %all-to-all-start = ((f32[64,4,128]{2,1,0:T(4,128)}), f32[64,4,128]{2,1,0:T(4,128)S(1)}, u32[]{:S(2)}, u32[]{:S(2)}) async-start(f32[64,4,128]{2,1,0:T(4,128)} %bitcast.16), calls=%async_computation | async-start | bytes 262144 | tf_op jit(solution)/shard_map/all_to_all | solution.py:350
  27.0 0.9 %copy_bitcast_fusion = f32[16,8,128]{2,0,1:T(8,128)S(1)} fusion(f32[16,1024]{1,0:T(8,128)} %rate_ref.1), kind=kLoop, calls=%fused_computation | loop fusion | flops 16384 | bytes 131072 | tf_op jit(solution)/shard_map/reshape | solution.py:381
  27.8 6.1 %all-to-all-done.ends_ref = f32[64,4,128]{2,1,0:T(4,128)S(1)} async-done(((f32[64,4,128]{2,1,0:T(4,128)}), f32[64,4,128]{2,1,0:T(4,128)S(1)}, u32[]{:S(2)}, u32[]{:S(2)}) %all-to-all-start) | async-done | bytes 131104 | tf_op jit(solution)/shard_map/all_to_all | solution.py:350
  33.9 0.8 %relay.1 = f32[64,4,128]{2,1,0:T(4,128)} custom-call(s32[1]{0:T(128)} %bitcast.share_ref, f32[64,4,128]{2,1,0:T(4,128)S(1)} %all-to-all-done.ends_ref, f32[128,128]{1,0:T(8,128)S(1)} %bitcast.13), custom_call_target="tpu_custom_call" | custom-call | tf_op jit(solution)/shard_map/relay/pallas_call | solution.py:386
  34.7 14.8 %all-to-all-start.1 = ((f32[64,4,128]{2,1,0:T(4,128)}), f32[64,4,128]{2,1,0:T(4,128)S(1)}, u32[]{:S(2)}, u32[]{:S(2)}) async-start(f32[64,4,128]{2,1,0:T(4,128)} %relay.1), calls=%async_computation.1 | async-start | bytes 262144 | tf_op jit(solution)/shard_map/all_to_all | solution.py:396
  49.5 0.9 %sqrt_multiply_fusion.weight_hbm = f32[16,1024]{1,0:T(8,128)S(1)} fusion(f32[16,1024]{1,0:T(8,128)} %param.8, f32[16,1024]{1,0:T(8,128)} %rate_ref.1), kind=kLoop, calls=%fused_computation.1 | loop fusion | flops 49152 | bytes 196608 | tf_op jit(solution)/shard_map/mul | solution.py:352
  50.5 0.0 copy-start
  50.5 0.8 %copy-done = f32[16,1024]{1,0:T(8,128)S(1)} copy-done((f32[16,1024]{1,0:T(8,128)S(1)}, f32[16,1024]{1,0:T(8,128)}, u32[]{:S(2)}) %copy-start) | copy-done | bytes 65560
  51.3 0.0 copy-start.3
  51.3 1.0 %copy-done.3 = bf16[256,1024]{1,0:T(8,128)(2,1)S(1)} copy-done((bf16[256,1024]{1,0:T(8,128)(2,1)S(1)}, bf16[256,1024]{1,0:T(8,128)(2,1)}, u32[]{:S(2)}) %copy-start.3) | copy-done | bytes 524312
  52.4 0.0 copy-start.4
  52.4 0.7 %copy-done.4 = f32[1024]{0:T(1024)S(1)} copy-done((f32[1024]{0:T(1024)S(1)}, f32[1024]{0:T(1024)}, u32[]{:S(2)}) %copy-start.4) | copy-done | bytes 4120
  53.0 0.0 copy-start.2
  53.0 5.2 %within_forward.1.refs_0_ = f32[2,384,1024]{2,1,0:T(8,128)S(1)} custom-call(bf16[256,1024]{1,0:T(8,128)(2,1)S(1)} %copy-done.3, f32[16,1024]{1,0:T(8,128)S(1)} %copy-done, f32[16,1024]{1,0:T(8,128)S(1)} %sqrt_multiply_fusion.weight_hbm, f32[1,1024]{1,0:T(1,128)S(1)} %bitcast.14), custom_call_target="tpu_custom_call" | custom-call | flops 25165824 | bytes 1572864 | tf_op jit(solution)/shard_map/within_forward/pallas_call | solution.py:357
  58.3 0.0 copy-done.5
  58.3 0.0 copy-done.2
  58.3 0.0 copy-start.1
  58.3 5.2 %within_backward.1.both_ref = f32[2,384,1024]{2,1,0:T(8,128)S(1)} custom-call(bf16[256,1024]{1,0:T(8,128)(2,1)S(1)} %copy-done.2, f32[16,1024]{1,0:T(8,128)S(1)} %copy-done, f32[16,1024]{1,0:T(8,128)S(1)} %sqrt_multiply_fusion.weight_hbm, f32[1,1024]{1,0:T(1,128)S(1)} %bitcast.15, ...), custom_call_target="tpu_custom_call", output_to_operand_aliasing={{}: (4, {})} | custom-call | flops 25165824 | bytes 1572864 | tf_op jit(solution)/shard_map/within_backward/pallas_call | solution.py:357
  63.6 0.0 all-to-all-done.1
  63.6 0.0 copy-done.1
  63.6 3.2 %carry.1 = (bf16[256,1024]{1,0:T(8,128)(2,1)}, bf16[256,1024]{1,0:T(8,128)(2,1)}) custom-call(f32[2,384,1024]{2,1,0:T(8,128)S(1)} %within_backward.1.both_ref, f32[16,1024]{1,0:T(8,128)S(1)} %copy-done.1, f32[2,128,128]{2,1,0:T(8,128)S(1)} %bitcast.12), custom_call_target="tpu_custom_call" | custom-call | tf_op jit(solution)/shard_map/carry/pallas_call | solution.py:398
Async XLA Ops:
  0.6 57.7 %copy-start.5 = (f32[1024]{0:T(1024)S(1)}, f32[1024]{0:T(1024)}, u32[]{:S(2)}) copy-start(f32[1024]{0:T(1024)} %param.9) | copy-start | bytes 12292
  5.3 28.6 %all-to-all-start = ((f32[64,4,128]{2,1,0:T(4,128)}), f32[64,4,128]{2,1,0:T(4,128)S(1)}, u32[]{:S(2)}, u32[]{:S(2)}) async-start(f32[64,4,128]{2,1,0:T(4,128)} %bitcast.16), calls=%async_computation | async-start | bytes 262144 | tf_op jit(solution)/shard_map/all_to_all | solution.py:350
  34.7 28.9 %all-to-all-start.1 = ((f32[64,4,128]{2,1,0:T(4,128)}), f32[64,4,128]{2,1,0:T(4,128)S(1)}, u32[]{:S(2)}, u32[]{:S(2)}) async-start(f32[64,4,128]{2,1,0:T(4,128)} %relay.1), calls=%async_computation.1 | async-start | bytes 262144 | tf_op jit(solution)/shard_map/all_to_all | solution.py:396
  50.5 0.8 %copy-start = (f32[16,1024]{1,0:T(8,128)S(1)}, f32[16,1024]{1,0:T(8,128)}, u32[]{:S(2)}) copy-start(f32[16,1024]{1,0:T(8,128)} %rate_ref.1) | copy-start | bytes 196612
  51.3 1.0 %copy-start.3 = (bf16[256,1024]{1,0:T(8,128)(2,1)S(1)}, bf16[256,1024]{1,0:T(8,128)(2,1)}, u32[]{:S(2)}) copy-start(bf16[256,1024]{1,0:T(8,128)(2,1)} %x_hbm) | copy-start | bytes 1572868
  52.4 0.7 %copy-start.4 = (f32[1024]{0:T(1024)S(1)}, f32[1024]{0:T(1024)}, u32[]{:S(2)}) copy-start(f32[1024]{0:T(1024)} %param.9) | copy-start | bytes 12292
  53.0 5.3 %copy-start.2 = (bf16[256,1024]{1,0:T(8,128)(2,1)S(1)}, bf16[256,1024]{1,0:T(8,128)(2,1)}, u32[]{:S(2)}) copy-start(bf16[256,1024]{1,0:T(8,128)(2,1)} %x_hbm.1) | copy-start | bytes 1572868
  58.3 5.3 %copy-start.1 = (f32[16,1024]{1,0:T(8,128)S(1)}, f32[16,1024]{1,0:T(8,128)}, u32[]{:S(2)}) copy-start(f32[16,1024]{1,0:T(8,128)} %rate_ref.1) | copy-start | bytes 196612

commit v5 on v4

--- a/solution.py
+++ b/solution.py
@@ -10,6 +10,7 @@
 LANES = 128
 F32 = jnp.float32
 ROOT, ROOT_OF = 41, 64
+PARTS = 2
 
 
 def row_of(table, n):
@@ -18,23 +19,6 @@
 
 def block_index():
     return lax.broadcasted_iota(jnp.int32, (SUB, LANES), 0)
-
-
-def blocked_position(x_ref, r, length):
-    return x_ref[pl.ds(r, SUB, stride=length), :]
-
-
-def block_ends(x_ref, decay, order, length):
-    ends = [None] * len(decay)
-    for step, r in enumerate(order):
-        x = blocked_position(x_ref, r, length)
-        for n in range(len(decay)):
-            ends[n] = x if step == 0 else decay[n] * ends[n] + x
-    return ends
-
-
-def orders(length):
-    return list(range(length)), list(range(length - 1, -1, -1))
 
 
 def summed_positions(parts):
@@ -131,26 +115,6 @@
     lax.fori_loop(0, width // (2 * LANES), both_columns, 0)
 
 
-def entering_states(ends, rate, length, forward):
-    block = block_index()
-    entering = []
-    for n in range(len(ends)):
-        total = ends[n]
-        reach = 1
-        while reach < SUB:
-            ratio = jnp.exp(-row_of(rate, n) * float(length * reach))
-            total = total + ratio * shifted_blocks(total, reach, block, forward)
-            reach *= 2
-        entering.append(shifted_blocks(total, 1, block, forward))
-    return entering
-
-
-def shifted_blocks(x, by, block, forward):
-    if forward:
-        return jnp.where(block >= by, pltpu.roll(x, by, 0), 0.0)
-    return jnp.where(block < SUB - by, pltpu.roll(x, SUB - by, 0), 0.0)
-
-
 def within_kernel(
     is_forward,
     x_hbm,
@@ -161,26 +125,29 @@
 ):
     (
         both_ref,
+        span_ref,
         whole_ref,
-        x_ref,
-        y_ref,
+        turned_ref,
         rate_ref,
         weight_ref,
         gain_ref,
+        decays_ref,
+        weights_ref,
+        gains_ref,
         sems,
         table_sems,
-    ) = refs[-9:]
+    ) = refs[-12:]
     local_ref = both_ref.at[0 if is_forward else 1]
     positions, width = whole_ref.shape
-    length = positions // SUB
     states = rate_ref.shape[0]
-    order = orders(length)[0 if is_forward else 1]
+    columns = width // LANES
+    pair = 2 * SUB
     place = block_index()
     distance = (place + 1 if is_forward else SUB - place).astype(F32)
 
     def part_copy(part):
-        lanes = pl.ds(pl.multiple_of(part * 2 * LANES, 2 * LANES), 2 * LANES)
-        return pltpu.make_async_copy(x_hbm.at[:, lanes], whole_ref.at[:, lanes], sems.at[part])
+        rows = pl.ds(part * (positions // PARTS), positions // PARTS)
+        return pltpu.make_async_copy(x_hbm.at[rows, :], whole_ref.at[rows, :], sems.at[part])
 
     table_copies = [
         pltpu.make_async_copy(hbm, ref, table_sems.at[i])
@@ -190,40 +157,49 @@
     ]
     for copy in table_copies:
         copy.start()
-    for part in range(width // (2 * LANES)):
+    for part in range(PARTS):
         part_copy(part).start()
     for copy in table_copies:
         copy.wait()
 
-    def column(c, _):
-        lanes = pl.ds(pl.multiple_of(c * LANES, LANES), LANES)
-        x_ref[...] = whole_ref[:, lanes].astype(F32)
+    for c in range(columns):
+        lanes = pl.ds(c * LANES, LANES)
         rate = rate_ref[:, lanes]
-        decay_table = jnp.exp(-rate)
-        decay = [row_of(decay_table, n) for n in range(states)]
-        weight_table = weight_ref[:, lanes]
-        weight = [row_of(weight_table, n) for n in range(states)]
-        gain = jnp.broadcast_to(gain_ref[:, lanes], (SUB, LANES))
+        weight = weight_ref[:, lanes]
+        span_ref[pl.ds(c * states, states), :] = jnp.exp(-rate * float(positions))
+        decays_ref[pl.ds(c, states, stride=columns), :] = jnp.exp(-rate)
+        weights_ref[pl.ds(c, states, stride=columns), :] = weight
+        gains_ref[pl.ds(c, 1), :] = gain_ref[:, lanes]
         for n in range(states):
             reach = jnp.exp(-row_of(rate, n) * distance)
-            local_ref[pl.ds(positions + n * SUB, SUB), lanes] = weight[n] * reach
-        ends = block_ends(x_ref, decay, order, length)
-        state = entering_states(ends, rate, length, is_forward)
-        for r in order:
-            x = blocked_position(x_ref, r, length)
+            local_ref[pl.ds(positions + n * SUB, SUB), lanes] = row_of(weight, n) * reach
+    decay = [decays_ref[n * columns : (n + 1) * columns, :] for n in range(states)]
+    weight = [weights_ref[n * columns : (n + 1) * columns, :] for n in range(states)]
+    gain = gains_ref[...]
+    for part in range(PARTS):
+        part_copy(part).wait()
+
+    def advance(step, state):
+        at = step if is_forward else positions // pair - 1 - step
+        start = pl.multiple_of(at * pair, pair)
+        for c in range(columns):
+            x = whole_ref[pl.ds(start, pair), c * LANES : (c + 1) * LANES]
+            turned_ref[pl.ds(c, pair, stride=columns), :] = x.astype(F32)
+        state = list(state)
+        for t in range(pair) if is_forward else range(pair - 1, -1, -1):
+            x = turned_ref[t * columns : (t + 1) * columns, :]
             terms = [gain * x]
             for n in range(states):
                 state[n] = decay[n] * state[n] + x
                 terms.append(weight[n] * state[n])
-            y_ref[pl.ds(r, SUB, stride=length), :] = added(terms)
-        local_ref[pl.ds(0, positions), lanes] = y_ref[...]
-        return 0
-
-    def both_columns(part, _):
-        part_copy(part).wait()
-        return lax.fori_loop(2 * part, 2 * part + 2, column, 0)
-
-    lax.fori_loop(0, width // (2 * LANES), both_columns, 0)
+            turned_ref[t * columns : (t + 1) * columns, :] = added(terms)
+        for c in range(columns):
+            y = turned_ref[pl.ds(c, pair, stride=columns), :]
+            local_ref[pl.ds(start, pair), c * LANES : (c + 1) * LANES] = y
+        return tuple(state)
+
+    zero = jnp.zeros((columns, LANES), F32)
+    lax.fori_loop(0, positions // pair, advance, (zero,) * states)
 
 
 def added(terms):
@@ -316,7 +292,7 @@
     in_vmem = pl.BlockSpec(memory_space=pltpu.VMEM)
     elements = positions * channels * states
     whole = pltpu.VMEM((positions, channels), signal.dtype)
-    column = pltpu.VMEM((positions, LANES), F32)
+    turned = pltpu.VMEM((states * columns, LANES), F32)
     table = pltpu.VMEM(decay_rate.shape, F32)
     copy_sems = pltpu.SemaphoreType.DMA((2, columns // 2))
 
@@ -357,17 +333,22 @@
         return pl.pallas_call(
             functools.partial(within_kernel, is_forward),
             in_specs=[in_hbm] * 4 + [in_vmem] * len(other),
-            out_specs=in_vmem,
-            out_shape=jax.ShapeDtypeStruct((2, depth, channels), F32),
+            out_specs=[in_vmem] * 2,
+            out_shape=[
+                jax.ShapeDtypeStruct((2, depth, channels), F32),
+                jax.ShapeDtypeStruct((columns * states, LANES), F32),
+            ],
             input_output_aliases={4: 0} if other else {},
             scratch_shapes=[
                 whole,
-                column,
-                column,
+                pltpu.VMEM((2 * SUB * columns, LANES), F32),
                 table,
                 table,
                 pltpu.VMEM((1, channels), F32),
-                pltpu.SemaphoreType.DMA((columns // 2,)),
+                turned,
+                turned,
+                pltpu.VMEM((columns, LANES), F32),
+                pltpu.SemaphoreType.DMA((PARTS,)),
                 pltpu.SemaphoreType.DMA((3,)),
             ],
             cost_estimate=pl.CostEstimate(
@@ -377,10 +358,8 @@
             name="within_forward" if is_forward else "within_backward",
         )(x, decay_rate, weight, gain, *other)
 
-    rate_then, _ = lax.optimization_barrier((decay_rate, ends))
-    span = jnp.exp(-float(positions) * rate_then).reshape(states, columns, LANES)
-    span = span.swapaxes(0, 1).reshape(columns * states, LANES)
-
+    half, span = within(True, signal)
+    both, _ = within(False, cotangent, half)
     share = lax.rem(lax.axis_index("seq") + (devices - first), devices)
     share = share.astype(jnp.int32).reshape(1)
     carried = pl.pallas_call(
@@ -391,8 +370,6 @@
         compiler_params=vmem(4),
         name="relay",
     )(share, gathered, span)
-    signal, cotangent, _ = lax.optimization_barrier((signal, cotangent, carried))
-    both = within(False, cotangent, within(True, signal))
     returned = exchanged(carried).reshape(2, columns * states, LANES)
 
     return pl.pallas_call(

time: 67.2 us -> 60.1 us (0.89)
  waiting for transfers between devices: 6.1 us -> 0.94 us
  Pallas kernels: 19.1 us -> 15.2 us
  local copies, waits for them, and re-layouts: 2.58 us -> 5.13 us
  other arithmetic: 1.78 us -> 0.92 us
    all_to_all x1, waiting for transfers between devices: 6.1 us -> 0.43 us  [shards(): gathered = exchanged(sent)]
    pallas_call x2, Pallas kernels: 10.5 us -> 6.56 us  [within(): pl.pallas_call(functools.partial(within_kernel, is_forward), in_specs=[in...]
    unnamed x12 -> x14, local copies, waits for them, and re-layouts: 2.58 us -> 5.13 us
    reshape x1 -> x0, other arithmetic: 0.86 us -> none  [shards(): jnp.exp(-float(positions) * rate_then).reshape(states, columns, LANES)]
  transfers between devices with their start and end apart: 2 -> 2, of which waited for: 1 -> 2; matrix products, arithmetic and copies ran while one was open for 3% -> 2% of each run, Pallas kernels for 16% -> 11%
where the time goes in v5:
time: 60.1 us; the launch traced here: 59.4 us
  starting transfers between devices  36.5 us (61%)
  Pallas kernels  15.2 us (25%)
  local copies, waits for them, and re-layouts  5.13 us (9%)
  waiting for transfers between devices  0.94 us (2%)
  other arithmetic  0.92 us (2%)
  between operations  0.71 us (1%)
    all_to_all x1, starting transfers between devices, shards(): gathered = exchanged(sent)  21.6 us
    all_to_all x1, starting transfers between devices, shards(): returned = exchanged(carried).reshape(2, columns * states, LANES)  14.8 us
    pallas_call x2, Pallas kernels, within(): pl.pallas_call(functools.partial(within_kernel, is_forward), in_specs=[in...  6.56 us
    unnamed x14, local copies, waits for them, and re-layouts  5.13 us
    pallas_call x1, Pallas kernels, shards(): pl.pallas_call(ends_kernel, in_specs=[in_hbm] * 3, out_specs=in_vmem, out...  4.68 us
    pallas_call x1, Pallas kernels, shards(): pl.pallas_call(carry_kernel, in_specs=[in_vmem] * 3, out_specs=[in_hbm] *...  3.18 us
  transfers between devices with their start and end apart: 2, of which 2 were waited for; matrix products, arithmetic and copies ran while one was open for 2% of the time, Pallas kernels for 11%

profile of v5, /device:TPU:24, one launch (start us, length us, event | category | flops | bytes accessed | tf_op | source)
XLA Modules:
  0.0 59.4 jit_solution(12207793196034379451)
XLA Ops:
  0.6 0.0 copy-start.4
  0.6 4.7 %ends.1 = f32[2,128,128]{2,1,0:T(8,128)} custom-call(bf16[256,1024]{1,0:T(8,128)(2,1)} %signal_hbm.1, bf16[256,1024]{1,0:T(8,128)(2,1)} %cotangent_hbm.1, f32[16,1024]{1,0:T(8,128)} %rate_ref.1), custom_call_target="tpu_custom_call" | custom-call | tf_op jit(solution)/shard_map/ends/pallas_call | solution.py:299
  5.3 21.6 %all-to-all-start = ((f32[64,4,128]{2,1,0:T(4,128)}), f32[64,4,128]{2,1,0:T(4,128)S(1)}, u32[]{:S(2)}, u32[]{:S(2)}) async-start(f32[64,4,128]{2,1,0:T(4,128)} %bitcast.7), calls=%async_computation | async-start | bytes 262144 | tf_op jit(solution)/shard_map/all_to_all | solution.py:326
  27.0 0.9 %sqrt_multiply_fusion.weight_hbm = f32[16,1024]{1,0:T(8,128)S(1)} fusion(f32[16,1024]{1,0:T(8,128)} %param.8, f32[16,1024]{1,0:T(8,128)} %rate_ref.1), kind=kLoop, calls=%fused_computation | loop fusion | flops 49152 | bytes 196608 | tf_op jit(solution)/shard_map/mul | solution.py:328
  27.9 0.0 copy-start
  27.9 1.0 %copy-done = bf16[256,1024]{1,0:T(8,128)(2,1)S(1)} copy-done((bf16[256,1024]{1,0:T(8,128)(2,1)S(1)}, bf16[256,1024]{1,0:T(8,128)(2,1)}, u32[]{:S(2)}) %copy-start) | copy-done | bytes 524312
  28.9 0.0 copy-start.2
  28.9 0.8 %copy-done.2 = f32[16,1024]{1,0:T(8,128)S(1)} copy-done((f32[16,1024]{1,0:T(8,128)S(1)}, f32[16,1024]{1,0:T(8,128)}, u32[]{:S(2)}) %copy-start.2) | copy-done | bytes 65560
  29.8 0.0 copy-start.5
  29.8 0.7 %copy-done.5 = f32[1024]{0:T(1024)S(1)} copy-done((f32[1024]{0:T(1024)S(1)}, f32[1024]{0:T(1024)}, u32[]{:S(2)}) %copy-start.5) | copy-done | bytes 4120
  30.5 3.0 %within_forward.1 = (f32[2,384,1024]{2,1,0:T(8,128)S(1)}, f32[128,128]{1,0:T(8,128)S(1)}) custom-call(bf16[256,1024]{1,0:T(8,128)(2,1)S(1)} %copy-done, f32[16,1024]{1,0:T(8,128)S(1)} %copy-done.2, f32[16,1024]{1,0:T(8,128)S(1)} %sqrt_multiply_fusion.weight_hbm, f32[1,1024]{1,0:T(1,128)S(1)} %bitcast.5), custom_call_target="tpu_custom_call" | custom-call | flops 25165824 | bytes 1572864 | tf_op jit(solution)/shard_map/within_forward/pallas_call | solution.py:333
  33.5 0.4 all-to-all-done.ends_ref
  33.9 0.8 %relay.1 = f32[64,4,128]{2,1,0:T(4,128)} custom-call(s32[1]{0:T(128)} %bitcast.1.share_ref, f32[64,4,128]{2,1,0:T(4,128)S(1)} %all-to-all-done.ends_ref, f32[128,128]{1,0:T(8,128)S(1)} %get-tuple-element.7.span_ref), custom_call_target="tpu_custom_call" | custom-call | tf_op jit(solution)/shard_map/relay/pallas_call | solution.py:365
  34.7 14.8 %all-to-all-start.1 = ((f32[64,4,128]{2,1,0:T(4,128)}), f32[64,4,128]{2,1,0:T(4,128)S(1)}, u32[]{:S(2)}, u32[]{:S(2)}) async-start(f32[64,4,128]{2,1,0:T(4,128)} %relay.1), calls=%async_computation.1 | async-start | bytes 262144 | tf_op jit(solution)/shard_map/all_to_all | solution.py:373
  49.6 0.0 copy-start.1
  49.6 1.0 %copy-done.1 = bf16[256,1024]{1,0:T(8,128)(2,1)S(1)} copy-done((bf16[256,1024]{1,0:T(8,128)(2,1)S(1)}, bf16[256,1024]{1,0:T(8,128)(2,1)}, u32[]{:S(2)}) %copy-start.1) | copy-done | bytes 524312
  50.6 0.0 copy-start.3
  50.6 0.8 %copy-done.3 = f32[16,1024]{1,0:T(8,128)S(1)} copy-done((f32[16,1024]{1,0:T(8,128)S(1)}, f32[16,1024]{1,0:T(8,128)}, u32[]{:S(2)}) %copy-start.3) | copy-done | bytes 65560
  51.5 0.0 copy-start.6
  51.5 0.7 %copy-done.6 = f32[1024]{0:T(1024)S(1)} copy-done((f32[1024]{0:T(1024)S(1)}, f32[1024]{0:T(1024)}, u32[]{:S(2)}) %copy-start.6) | copy-done | bytes 4120
  52.1 3.5 %within_backward.1 = (f32[2,384,1024]{2,1,0:T(8,128)S(1)}, f32[128,128]{1,0:T(8,128)}) custom-call(bf16[256,1024]{1,0:T(8,128)(2,1)S(1)} %copy-done.1, f32[16,1024]{1,0:T(8,128)S(1)} %copy-done.3, f32[16,1024]{1,0:T(8,128)S(1)} %sqrt_multiply_fusion.weight_hbm, f32[1,1024]{1,0:T(1,128)S(1)} %bitcast.6, ...), custom_call_target="tpu_custom_call", output_to_operand_aliasing={{0}: (4, {})} | custom-call | flops 25165824 | bytes 1572864 | tf_op jit(solution)/shard_map/within_backward/pallas_call | solution.py:333
  55.7 0.5 all-to-all-done.1
  56.2 0.0 copy-done.4
  56.2 3.2 %carry.1 = (bf16[256,1024]{1,0:T(8,128)(2,1)}, bf16[256,1024]{1,0:T(8,128)(2,1)}) custom-call(f32[2,384,1024]{2,1,0:T(8,128)S(1)} %get-tuple-element.6.both_ref, f32[16,1024]{1,0:T(8,128)S(1)} %copy-done.4, f32[2,128,128]{2,1,0:T(8,128)S(1)} %bitcast.4), custom_call_target="tpu_custom_call" | custom-call | tf_op jit(solution)/shard_map/carry/pallas_call | solution.py:375
Async XLA Ops:
  0.6 55.6 %copy-start.4 = (f32[16,1024]{1,0:T(8,128)S(1)}, f32[16,1024]{1,0:T(8,128)}, u32[]{:S(2)}) copy-start(f32[16,1024]{1,0:T(8,128)} %rate_ref.1) | copy-start | bytes 196612
  5.3 28.6 %all-to-all-start = ((f32[64,4,128]{2,1,0:T(4,128)}), f32[64,4,128]{2,1,0:T(4,128)S(1)}, u32[]{:S(2)}, u32[]{:S(2)}) async-start(f32[64,4,128]{2,1,0:T(4,128)} %bitcast.7), calls=%async_computation | async-start | bytes 262144 | tf_op jit(solution)/shard_map/all_to_all | solution.py:326
  27.9 1.0 %copy-start = (bf16[256,1024]{1,0:T(8,128)(2,1)S(1)}, bf16[256,1024]{1,0:T(8,128)(2,1)}, u32[]{:S(2)}) copy-start(bf16[256,1024]{1,0:T(8,128)(2,1)} %signal_hbm.1) | copy-start | bytes 1572868
  28.9 0.8 %copy-start.2 = (f32[16,1024]{1,0:T(8,128)S(1)}, f32[16,1024]{1,0:T(8,128)}, u32[]{:S(2)}) copy-start(f32[16,1024]{1,0:T(8,128)} %rate_ref.1) | copy-start | bytes 196612
  29.8 0.7 %copy-start.5 = (f32[1024]{0:T(1024)S(1)}, f32[1024]{0:T(1024)}, u32[]{:S(2)}) copy-start(f32[1024]{0:T(1024)} %param.9) | copy-start | bytes 12292
  34.7 21.5 %all-to-all-start.1 = ((f32[64,4,128]{2,1,0:T(4,128)}), f32[64,4,128]{2,1,0:T(4,128)S(1)}, u32[]{:S(2)}, u32[]{:S(2)}) async-start(f32[64,4,128]{2,1,0:T(4,128)} %relay.1), calls=%async_computation.1 | async-start | bytes 262144 | tf_op jit(solution)/shard_map/all_to_all | solution.py:373
  49.6 1.0 %copy-start.1 = (bf16[256,1024]{1,0:T(8,128)(2,1)S(1)}, bf16[256,1024]{1,0:T(8,128)(2,1)}, u32[]{:S(2)}) copy-start(bf16[256,1024]{1,0:T(8,128)(2,1)} %cotangent_hbm.1) | copy-start | bytes 1572868
  50.6 0.8 %copy-start.3 = (f32[16,1024]{1,0:T(8,128)S(1)}, f32[16,1024]{1,0:T(8,128)}, u32[]{:S(2)}) copy-start(f32[16,1024]{1,0:T(8,128)} %rate_ref.1) | copy-start | bytes 196612
  51.5 0.7 %copy-start.6 = (f32[1024]{0:T(1024)S(1)}, f32[1024]{0:T(1024)}, u32[]{:S(2)}) copy-start(f32[1024]{0:T(1024)} %param.9) | copy-start | bytes 12292

commit v6 on v5

v6 whole, which is shorter than its diff:
```python
import functools
import jax
import jax.numpy as jnp
from jax import lax
from jax.experimental import pallas as pl
from jax.experimental.pallas import tpu as pltpu
from jax.sharding import PartitionSpec as P

PARTS = 4
SUB = 8
LANES = 128
F32 = jnp.float32


def row_of(table, n):
    return jnp.broadcast_to(table[n : n + 1, :], (SUB, LANES))


def block_index():
    return lax.broadcasted_iota(jnp.int32, (SUB, LANES), 0)


def ends_kernel(
    signal_hbm,
    cotangent_hbm,
    rate_hbm,
    ends_ref,
    signal_ref,
    cotangent_ref,
    rate_ref,
    turned_ref,
    decays_ref,
    sems,
    rate_sem,
):
    positions, width = signal_ref.shape
    states = rate_ref.shape[0]
    columns = width // LANES
    pair = 2 * SUB
    share = positions // PARTS

    def part_copies(part):
        copies = []
        for side, (hbm, ref) in enumerate(
            ((signal_hbm, signal_ref), (cotangent_hbm, cotangent_ref))
        ):
            at = part if side == 0 else PARTS - 1 - part
            rows = pl.ds(pl.multiple_of(at * share, share), share)
            copies.append(
                pltpu.make_async_copy(hbm.at[rows, :], ref.at[rows, :], sems.at[side, part])
            )
        return copies

    rate_copy = pltpu.make_async_copy(rate_hbm, rate_ref, rate_sem)
    rate_copy.start()
    for part in range(PARTS):
        for copy in part_copies(part):
            copy.start()
    rate_copy.wait()
    for c in range(columns):
        rate = rate_ref[:, c * LANES : (c + 1) * LANES]
        decays_ref[pl.ds(c, states, stride=columns), :] = jnp.exp(-rate)
    decay = [decays_ref[n * columns : (n + 1) * columns, :] for n in range(states)]

    def advance(step, state):
        start = pl.multiple_of(step * pair, pair)
        last = pl.multiple_of(positions - pair - step * pair, pair)
        for c in range(columns):
            lanes = pl.ds(c * LANES, LANES)
            x = signal_ref[pl.ds(start, pair), lanes]
            turned_ref[0, pl.ds(c, pair, stride=columns), :] = x.astype(F32)
            g = cotangent_ref[pl.ds(last, pair), lanes]
            turned_ref[1, pl.ds(c, pair, stride=columns), :] = g.astype(F32)
        ends, starts = list(state[0]), list(state[1])
        for t in range(pair):
            x = turned_ref[0, t * columns : (t + 1) * columns, :]
            back = pair - 1 - t
            g = turned_ref[1, back * columns : (back + 1) * columns, :]
            for n in range(states):
                ends[n] = decay[n] * ends[n] + x
                starts[n] = decay[n] * starts[n] + g
        return tuple(ends), tuple(starts)

    def part_of(part, state):
        for copy in part_copies(part):
            copy.wait()
        steps = share // pair
        return lax.fori_loop(part * steps, (part + 1) * steps, advance, state)

    zero = (jnp.zeros((columns, LANES), F32),) * states
    sums = lax.fori_loop(0, PARTS, part_of, (zero, zero))
    for side in range(2):
        for n in range(states):
            ends_ref[side, n * columns : (n + 1) * columns, :] = sums[side][n]


def within_kernel(is_forward, x_ref, table_ref, *refs):
    both_ref, turned_ref, decays_ref, weights_ref, gains_ref = refs[-5:]
    local_ref = both_ref.at[0 if is_forward else 1]
    positions, width = x_ref.shape
    states = (table_ref.shape[0] - 1) // 2
    columns = width // LANES
    pair = 2 * SUB
    place = block_index()
    distance = (place + 1 if is_forward else SUB - place).astype(F32)

    for c in range(columns):
        lanes = pl.ds(c * LANES, LANES)
        rate = table_ref[:states, lanes]
        weight = table_ref[states : 2 * states, lanes]
        decays_ref[pl.ds(c, states, stride=columns), :] = jnp.exp(-rate)
        weights_ref[pl.ds(c, states, stride=columns), :] = weight
        gains_ref[pl.ds(c, 1), :] = table_ref[2 * states :, lanes]
        for n in range(states):
            reach = jnp.exp(-row_of(rate, n) * distance)
            local_ref[pl.ds(positions + n * SUB, SUB), lanes] = row_of(weight, n) * reach
    decay = [decays_ref[n * columns : (n + 1) * columns, :] for n in range(states)]
    weight = [weights_ref[n * columns : (n + 1) * columns, :] for n in range(states)]
    gain = gains_ref[...]

    def advance(step, state):
        at = step if is_forward else positions // pair - 1 - step
        start = pl.multiple_of(at * pair, pair)
        for c in range(columns):
            x = x_ref[pl.ds(start, pair), c * LANES : (c + 1) * LANES]
            turned_ref[pl.ds(c, pair, stride=columns), :] = x.astype(F32)
        state = list(state)
        for t in range(pair) if is_forward else range(pair - 1, -1, -1):
            x = turned_ref[t * columns : (t + 1) * columns, :]
            terms = [gain * x]
            for n in range(states):
                state[n] = decay[n] * state[n] + x
                terms.append(weight[n] * state[n])
            turned_ref[t * columns : (t + 1) * columns, :] = added(terms)
        for c in range(columns):
            y = turned_ref[pl.ds(c, pair, stride=columns), :]
            local_ref[pl.ds(start, pair), c * LANES : (c + 1) * LANES] = y
        return tuple(state)

    zero = jnp.zeros((columns, LANES), F32)
    lax.fori_loop(0, positions // pair, advance, (zero,) * states)


def added(terms):
    while len(terms) > 1:
        terms = [
            terms[i] + terms[i + 1] if i + 1 < len(terms) else terms[i]
            for i in range(0, len(terms), 2)
        ]
    return terms[0]


class Layout:
    def __init__(self, devices):
        self.lows = 4
        self.lines = max(2, devices // 16)
        self.highs = devices // (self.lows * self.lines)
        self.members = self.lines * self.lows
        self.middle = self.highs // 2
        self.first = self.lines // 2 * self.lows + 1


    def member_groups(self):
        return [
            [
                m // self.lows * self.highs * self.lows + high * self.lows + m % self.lows
                for m in ((self.first + i) % self.members for i in range(self.members))
            ]
            for high in range(self.highs)
        ]

    def peer_groups(self):
        return [
            [
                (line * self.highs + (self.middle + i) % self.highs) * self.lows + low
                for i in range(self.highs)
            ]
            for line in range(self.lines)
            for low in range(self.lows)
        ]

    def place(self, index):
        high = lax.rem(index // self.lows, self.highs)
        line = index // (self.lows * self.highs)
        return high, self.slot(line, lax.rem(index, self.lows))

    def slot(self, line, low):
        member = line * self.lows + low
        return lax.rem(member + (self.members - self.first), self.members)


def share_of(layout, index_ref, span_ref, rows):
    high, share = layout.place(index_ref[0])
    half = layout.members // 2
    at = pl.multiple_of(lax.rem(share, half) * rows, rows)
    return high, share < half, span_ref[pl.ds(at, rows), :]


def totals_kernel(layout, index_ref, ends_ref, span_ref, totals_ref):
    rows = ends_ref.shape[1]
    _, forward, span = share_of(layout, index_ref, span_ref, rows)
    for line in range(layout.lines):
        total = None
        for step in range(layout.lows):
            low = jnp.where(forward, step, layout.lows - 1 - step)
            end = ends_ref[layout.slot(line, low)]
            total = end if total is None else span * total + end
        for peer in range(layout.highs):
            totals_ref[peer, line] = total


def relay_kernel(layout, index_ref, ends_ref, totals_ref, span_ref, carried_ref):
    rows = ends_ref.shape[1]
    high, forward, span = share_of(layout, index_ref, span_ref, rows)
    stride = span
    for _ in range(layout.lows - 1):
        stride = stride * span
    state = jnp.zeros(span.shape, F32)
    for line_step in range(layout.lines):
        line = jnp.where(forward, line_step, layout.lines - 1 - line_step)
        entering = state
        for high_step in range(layout.highs):
            this = jnp.where(forward, high_step, layout.highs - 1 - high_step)
            entering = jnp.where(this == high, state, entering)
            peer = lax.rem(this + layout.highs - layout.middle, layout.highs)
            state = stride * state + totals_ref[peer, line]
        for step in range(layout.lows):
            low = jnp.where(forward, step, layout.lows - 1 - step)
            at = layout.slot(line, low)
            carried_ref[at] = entering
            entering = span * entering + ends_ref[at]


def carry_kernel(
    both_ref, rate_ref, carried_ref, out_hbm, grad_hbm, out_ref, grad_ref, sems
):
    positions, width = out_ref.shape
    states = rate_ref.shape[0]
    tiles = positions // SUB

    def part_copies(part):
        lanes = pl.ds(pl.multiple_of(part * 2 * LANES, 2 * LANES), 2 * LANES)
        return [
            pltpu.make_async_copy(ref.at[:, lanes], hbm.at[:, lanes], sems.at[side, part])
            for side, (hbm, ref) in enumerate(((out_hbm, out_ref), (grad_hbm, grad_ref)))
        ]

    def column(c, _):
        lanes = pl.ds(pl.multiple_of(c * LANES, LANES), LANES)
        decay_table = jnp.exp(-rate_ref[:, lanes] * float(SUB))
        decay = [row_of(decay_table, n) for n in range(states)]
        rows = pl.ds(c, states, stride=width // LANES)
        for side, result in enumerate((out_ref, grad_ref)):
            local_ref = both_ref.at[side]
            carried = carried_ref[side, rows, :]
            terms = [
                local_ref[pl.ds(positions + n * SUB, SUB), lanes] * row_of(carried, n)
                for n in range(states)
            ]
            for pair in range(tiles // 2):
                halves = []
                first = pair * 2 * SUB if side == 0 else positions - (pair + 1) * 2 * SUB
                for half in range(2):
                    if pair or half:
                        terms = [decay[n] * terms[n] for n in range(states)]
                    start = first + (half if side == 0 else 1 - half) * SUB
                    local = local_ref[pl.ds(start, SUB), lanes]
                    halves.append(added(terms) + local)
                if side:
                    halves.reverse()
                both = jnp.concatenate(halves, axis=0)
                result[first : first + 2 * SUB, lanes] = both.astype(result.dtype)
        return 0

    def both_columns(part, _):
        lax.fori_loop(2 * part, 2 * part + 2, column, 0)
        for copy in part_copies(part):
            copy.start()
        return 0

    lax.fori_loop(0, width // (2 * LANES), both_columns, 0)
    for part in range(width // (2 * LANES)):
        for copy in part_copies(part):
            copy.wait()


def vmem(mib):
    return pltpu.CompilerParams(vmem_limit_bytes=mib << 20)


def shards(signal, cotangent, decay_rate, residue, skip_gain):
    positions, channels = signal.shape
    states = decay_rate.shape[0]
    columns = channels // LANES
    devices = lax.axis_size("seq")
    anywhere = pl.BlockSpec(memory_space=pl.ANY)
    in_hbm = pl.BlockSpec(memory_space=pltpu.HBM)
    in_vmem = pl.BlockSpec(memory_space=pltpu.VMEM)
    elements = positions * channels * states
    whole = pltpu.VMEM((positions, channels), signal.dtype)
    turned = pltpu.VMEM((states * columns, LANES), F32)
    copy_sems = pltpu.SemaphoreType.DMA((2, columns // 2))

    ends = pl.pallas_call(
        ends_kernel,
        in_specs=[in_hbm] * 3,
        out_specs=in_vmem,
        out_shape=jax.ShapeDtypeStruct((2, columns * states, LANES), F32),
        scratch_shapes=[
            whole,
            whole,
            pltpu.VMEM(decay_rate.shape, F32),
            pltpu.VMEM((2, 2 * SUB * columns, LANES), F32),
            turned,
            pltpu.SemaphoreType.DMA((2, PARTS)),
            pltpu.SemaphoreType.DMA,
        ],
        compiler_params=vmem(56),
        name="ends",
    )(signal, cotangent, decay_rate)

    layout = Layout(devices)
    rows = 2 * columns * states // layout.members
    index = lax.axis_index("seq").astype(jnp.int32).reshape(1)
    in_smem = pl.BlockSpec(memory_space=pltpu.SMEM)

    def exchanged(x, groups):
        return lax.all_to_all(x, "seq", 0, 0, axis_index_groups=groups)

    gathered = exchanged(ends.reshape(layout.members, rows, LANES), layout.member_groups())
    rate_then, _ = lax.optimization_barrier((decay_rate, ends))
    span = jnp.exp(-float(positions) * rate_then).reshape(states * columns, LANES)
    weight = residue * jnp.sqrt(-jnp.expm1(-2.0 * rate_then))
    tables = jnp.concatenate([rate_then, weight, skip_gain.reshape(1, channels)], axis=0)
    span, tables = lax.optimization_barrier((span, tables))
    totals = pl.pallas_call(
        functools.partial(totals_kernel, layout),
        in_specs=[in_smem, in_vmem, in_vmem],
        out_specs=in_vmem,
        out_shape=jax.ShapeDtypeStruct((layout.highs, layout.lines, rows, LANES), F32),
        compiler_params=vmem(4),
        name="totals",
    )(index, gathered, span)
    peers = exchanged(totals, layout.peer_groups())

    depth = positions + states * SUB

    def within(is_forward, x, *other):
        return pl.pallas_call(
            functools.partial(within_kernel, is_forward),
            in_specs=[in_vmem] * (2 + len(other)),
            out_specs=in_vmem,
            out_shape=jax.ShapeDtypeStruct((2, depth, channels), F32),
            input_output_aliases={2: 0} if other else {},
            scratch_shapes=[
                pltpu.VMEM((2 * SUB * columns, LANES), F32),
                turned,
                turned,
                pltpu.VMEM((columns, LANES), F32),
            ],
            cost_estimate=pl.CostEstimate(
                flops=6 * elements, bytes_accessed=6 * positions * channels, transcendentals=0
            ),
            compiler_params=vmem(8),
            name="within_forward" if is_forward else "within_backward",
        )(x, tables, *other)

    signal, _ = lax.optimization_barrier((signal, totals))
    half = within(True, signal)
    span, half = lax.optimization_barrier((span, half))

    carried = pl.pallas_call(
        functools.partial(relay_kernel, layout),
        in_specs=[in_smem] + [in_vmem] * 3,
        out_specs=in_vmem,
        out_shape=jax.ShapeDtypeStruct((layout.members, rows, LANES), F32),
        compiler_params=vmem(56),
        name="relay",
    )(index, gathered, peers, span)
    cotangent, _ = lax.optimization_barrier((cotangent, carried))
    both = within(False, cotangent, half)
    returned = exchanged(carried, layout.member_groups())
    returned = returned.reshape(2, columns * states, LANES)

    return pl.pallas_call(
        carry_kernel,
        in_specs=[in_vmem] * 3,
        out_specs=[in_hbm] * 2,
        out_shape=[jax.ShapeDtypeStruct(signal.shape, signal.dtype)] * 2,
        scratch_shapes=[whole, whole, copy_sems],
        compiler_params=vmem(8),
        name="carry",
    )(both, decay_rate, returned)


def solution(mesh):
    in_specs = (P("seq", "chan"), P("seq", "chan"), P(None, "chan"), P(None, "chan"), P("chan"))
    out_specs = (P("seq", "chan"), P("seq", "chan"))
    return jax.shard_map(
        lambda *arrays: tuple(shards(*arrays)),
        mesh=mesh,
        in_specs=in_specs,
        out_specs=out_specs,
        check_vma=False,
    )
```

time: 60.1 us -> 58.9 us (0.980)
  starting transfers between devices: 36.5 us -> 30.8 us
  waiting for transfers between devices: 0.94 us -> 6.42 us
  local copies, waits for them, and re-layouts: 5.13 us -> 2.11 us
  Pallas kernels: 15.2 us -> 16.4 us
  other arithmetic: 0.92 us -> 1.82 us
    all_to_all x2 -> x3, starting transfers between devices: 36.5 us -> 30.8 us  [exchanged(): return lax.all_to_all(x, 'seq', 0, 0, axis_index_groups=groups)]
    all_to_all x2 -> x3, waiting for transfers between devices: 0.94 us -> 6.42 us  [exchanged(): return lax.all_to_all(x, 'seq', 0, 0, axis_index_groups=groups)]
    unnamed x14 -> x10, local copies, waits for them, and re-layouts: 5.13 us -> 2.09 us
    pallas_call x1 -> x2, Pallas kernels: 0.79 us -> 2.37 us  [the longest x1 1.68 us: shards(): pl.pallas_call(functools.partial(relay_kernel, layout), in_specs=[in_smem...]
    pallas_call x2, Pallas kernels: 6.56 us -> 5.6 us  [within(): pl.pallas_call(functools.partial(within_kernel, is_forward), in_specs=[in...]
    concatenate x0 -> x1, other arithmetic: none -> 0.89 us  [shards(): jnp.concatenate([rate_then, weight, skip_gain.reshape(1, channels)], axis=0)]
  transfers between devices with their start and end apart: 2 -> 3, of which waited for: 2 -> 3; matrix products, arithmetic and copies ran while one was open for 2% -> 3% of each run, Pallas kernels for 11% -> 10%
where the time goes in v6:
time: 58.9 us; the launch traced here: 58.3 us
  starting transfers between devices  30.8 us (52%)
  Pallas kernels  16.4 us (28%)
  waiting for transfers between devices  6.42 us (11%)
  local copies, waits for them, and re-layouts  2.11 us (4%)
  other arithmetic  1.82 us (3%)
  between operations  0.68 us (1%)
    all_to_all x3, starting transfers between devices, exchanged(): return lax.all_to_all(x, 'seq', 0, 0, axis_index_groups=groups)  30.8 us
    all_to_all x3, waiting for transfers between devices, exchanged(): return lax.all_to_all(x, 'seq', 0, 0, axis_index_groups=groups)  6.42 us
    pallas_call x2, Pallas kernels, within(): pl.pallas_call(functools.partial(within_kernel, is_forward), in_specs=[in...  5.6 us
    pallas_call x1, Pallas kernels, shards(): pl.pallas_call(ends_kernel, in_specs=[in_hbm] * 3, out_specs=in_vmem, out...  5.27 us
    pallas_call x1, Pallas kernels, shards(): pl.pallas_call(carry_kernel, in_specs=[in_vmem] * 3, out_specs=[in_hbm] *...  3.2 us
    unnamed x10, local copies, waits for them, and re-layouts  2.09 us
    pallas_call x1, Pallas kernels, shards(): pl.pallas_call(functools.partial(relay_kernel, layout), in_specs=[in_smem...  1.68 us
  transfers between devices with their start and end apart: 3, of which 3 were waited for; matrix products, arithmetic and copies ran while one was open for 3% of the time, Pallas kernels for 10%

profile of v6, /device:TPU:24, one launch (start us, length us, event | category | flops | bytes accessed | tf_op | source)
XLA Modules:
  0.0 58.3 jit_solution(9422974466064955100)
XLA Ops:
  0.6 5.3 %ends.1 = f32[2,128,128]{2,1,0:T(8,128)} custom-call(bf16[256,1024]{1,0:T(8,128)(2,1)} %x_ref, bf16[256,1024]{1,0:T(8,128)(2,1)} %x_ref.1, f32[16,1024]{1,0:T(8,128)} %rate_ref.1), custom_call_target="tpu_custom_call" | custom-call | tf_op jit(solution)/shard_map/ends/pallas_call | solution.py:304
  5.9 9.6 %all-to-all-start = ((f32[16,16,128]{2,1,0:T(8,128)}), f32[16,16,128]{2,1,0:T(8,128)S(1)}, u32[]{:S(2)}, u32[]{:S(2)}) async-start(f32[16,16,128]{2,1,0:T(8,128)} %bitcast.5), calls=%async_computation | async-start | bytes 262144 | tf_op jit(solution)/shard_map/all_to_all | solution.py:328
  15.5 0.9 %sqrt_multiply_fusion = (f32[16,1024]{1,0:T(8,128)S(1)}, f32[16,1024]{1,0:T(8,128)S(1)}) fusion(f32[16,1024]{1,0:T(8,128)} %param.8, f32[16,1024]{1,0:T(8,128)} %rate_ref.1), kind=kLoop, calls=%fused_computation.1 | loop fusion | flops 65536 | bytes 262144 | tf_op jit(solution)/shard_map/mul | solution.py:333
  16.4 0.0 copy-start.4
  16.5 0.9 %pad_maximum_fusion.table_ref = f32[33,1024]{1,0:T(8,128)S(1)} fusion(f32[1,1024]{1,0:T(1,128)} %bitcast.6, f32[16,1024]{1,0:T(8,128)S(1)} %get-tuple-element.16, f32[16,1024]{1,0:T(8,128)} %rate_ref.1), kind=kLoop, calls=%fused_computation | loop fusion | flops 67584 | bytes 270336 | tf_op jit(solution)/shard_map/concatenate | solution.py:334
  17.4 3.1 %all-to-all-done.ends_ref = f32[16,16,128]{2,1,0:T(8,128)S(1)} async-done(((f32[16,16,128]{2,1,0:T(8,128)}), f32[16,16,128]{2,1,0:T(8,128)S(1)}, u32[]{:S(2)}, u32[]{:S(2)}) %all-to-all-start) | async-done | bytes 131104 | tf_op jit(solution)/shard_map/all_to_all | solution.py:328
  20.5 0.0 copy-start.2
  20.5 0.7 %totals.1 = f32[4,4,16,128]{3,2,1,0:T(8,128)} custom-call(s32[1]{0:T(128)} %bitcast.index_ref, f32[16,16,128]{2,1,0:T(8,128)S(1)} %all-to-all-done.ends_ref, f32[128,128]{1,0:T(8,128)S(1)} %reshape.21.span_ref), custom_call_target="tpu_custom_call" | custom-call | tf_op jit(solution)/shard_map/totals/pallas_call | solution.py:336
  21.2 15.0 %all-to-all-start.1 = ((f32[4,4,16,128]{3,2,1,0:T(8,128)}), f32[4,4,16,128]{3,2,1,0:T(8,128)}, u32[]{:S(2)}, u32[]{:S(2)}) async-start(f32[4,4,16,128]{3,2,1,0:T(8,128)} %totals.1), calls=%async_computation.1 | async-start | bytes 262144 | tf_op jit(solution)/shard_map/all_to_all | solution.py:328
  36.2 0.0 copy-start
  36.2 1.0 %copy-done = bf16[256,1024]{1,0:T(8,128)(2,1)S(1)} copy-done((bf16[256,1024]{1,0:T(8,128)(2,1)S(1)}, bf16[256,1024]{1,0:T(8,128)(2,1)}, u32[]{:S(2)}) %copy-start) | copy-done | bytes 524312
  37.2 2.8 %within_forward.1.refs_0_ = f32[2,384,1024]{2,1,0:T(8,128)S(1)} custom-call(bf16[256,1024]{1,0:T(8,128)(2,1)S(1)} %copy-done, f32[33,1024]{1,0:T(8,128)S(1)} %pad_maximum_fusion.table_ref), custom_call_target="tpu_custom_call" | custom-call | flops 25165824 | bytes 1572864 | tf_op jit(solution)/shard_map/within_forward/pallas_call | solution.py:349
  40.0 2.2 %all-to-all-done.1.totals_ref = f32[4,4,16,128]{3,2,1,0:T(8,128)} async-done(((f32[4,4,16,128]{3,2,1,0:T(8,128)}), f32[4,4,16,128]{3,2,1,0:T(8,128)}, u32[]{:S(2)}, u32[]{:S(2)}) %all-to-all-start.1) | async-done | bytes 131104 | tf_op jit(solution)/shard_map/all_to_all | solution.py:328
  42.2 0.0 copy-done.4
  42.2 0.0 copy-done.2
  42.2 1.7 %relay.1 = f32[16,16,128]{2,1,0:T(8,128)} custom-call(s32[1]{0:T(128)} %bitcast.index_ref, f32[16,16,128]{2,1,0:T(8,128)} %copy-done.2, f32[4,4,16,128]{3,2,1,0:T(8,128)} %all-to-all-done.1.totals_ref, f32[128,128]{1,0:T(8,128)} %copy-done.4), custom_call_target="tpu_custom_call" | custom-call | tf_op jit(solution)/shard_map/relay/pallas_call | solution.py:372
  43.9 6.2 %all-to-all-start.2 = ((f32[16,16,128]{2,1,0:T(8,128)}), f32[16,16,128]{2,1,0:T(8,128)S(1)}, u32[]{:S(2)}, u32[]{:S(2)}) async-start(f32[16,16,128]{2,1,0:T(8,128)} %relay.1), calls=%async_computation.2 | async-start | bytes 262144 | tf_op jit(solution)/shard_map/all_to_all | solution.py:328
  50.1 0.0 copy-start.1
  50.1 1.0 %copy-done.1 = bf16[256,1024]{1,0:T(8,128)(2,1)S(1)} copy-done((bf16[256,1024]{1,0:T(8,128)(2,1)S(1)}, bf16[256,1024]{1,0:T(8,128)(2,1)}, u32[]{:S(2)}) %copy-start.1) | copy-done | bytes 524312
  51.2 0.0 copy-start.3
  51.2 2.8 %within_backward.1.both_ref = f32[2,384,1024]{2,1,0:T(8,128)S(1)} custom-call(bf16[256,1024]{1,0:T(8,128)(2,1)S(1)} %copy-done.1, f32[33,1024]{1,0:T(8,128)S(1)} %pad_maximum_fusion.table_ref, f32[2,384,1024]{2,1,0:T(8,128)S(1)} %within_forward.1.refs_0_), custom_call_target="tpu_custom_call", output_to_operand_aliasing={{}: (2, {})} | custom-call | flops 25165824 | bytes 1572864 | tf_op jit(solution)/shard_map/within_backward/pallas_call | solution.py:349
  54.0 1.1 %all-to-all-done.2 = f32[16,16,128]{2,1,0:T(8,128)S(1)} async-done(((f32[16,16,128]{2,1,0:T(8,128)}), f32[16,16,128]{2,1,0:T(8,128)S(1)}, u32[]{:S(2)}, u32[]{:S(2)}) %all-to-all-start.2) | async-done | bytes 131104 | tf_op jit(solution)/shard_map/all_to_all | solution.py:328
  55.1 0.0 copy-done.3
  55.1 3.2 %carry.1 = (bf16[256,1024]{1,0:T(8,128)(2,1)}, bf16[256,1024]{1,0:T(8,128)(2,1)}) custom-call(f32[2,384,1024]{2,1,0:T(8,128)S(1)} %within_backward.1.both_ref, f32[16,1024]{1,0:T(8,128)S(1)} %copy-done.3, f32[2,128,128]{2,1,0:T(8,128)S(1)} %bitcast.4), custom_call_target="tpu_custom_call" | custom-call | tf_op jit(solution)/shard_map/carry/pallas_call | solution.py:385
  (1 shorter events, 0.0 us)
Async XLA Ops:
  5.9 14.6 %all-to-all-start = ((f32[16,16,128]{2,1,0:T(8,128)}), f32[16,16,128]{2,1,0:T(8,128)S(1)}, u32[]{:S(2)}, u32[]{:S(2)}) async-start(f32[16,16,128]{2,1,0:T(8,128)} %bitcast.5), calls=%async_computation | async-start | bytes 262144 | tf_op jit(solution)/shard_map/all_to_all | solution.py:328
  16.4 25.8 %copy-start.4 = (f32[128,128]{1,0:T(8,128)}, f32[128,128]{1,0:T(8,128)S(1)}, u32[]{:S(2)}) copy-start(f32[128,128]{1,0:T(8,128)S(1)} %reshape.21.span_ref) | copy-start | bytes 196612
  20.5 21.7 %copy-start.2 = (f32[16,16,128]{2,1,0:T(8,128)}, f32[16,16,128]{2,1,0:T(8,128)S(1)}, u32[]{:S(2)}) copy-start(f32[16,16,128]{2,1,0:T(8,128)S(1)} %all-to-all-done.ends_ref) | copy-start | bytes 393220
  21.2 21.0 %all-to-all-start.1 = ((f32[4,4,16,128]{3,2,1,0:T(8,128)}), f32[4,4,16,128]{3,2,1,0:T(8,128)}, u32[]{:S(2)}, u32[]{:S(2)}) async-start(f32[4,4,16,128]{3,2,1,0:T(8,128)} %totals.1), calls=%async_computation.1 | async-start | bytes 262144 | tf_op jit(solution)/shard_map/all_to_all | solution.py:328
  36.2 1.0 %copy-start = (bf16[256,1024]{1,0:T(8,128)(2,1)S(1)}, bf16[256,1024]{1,0:T(8,128)(2,1)}, u32[]{:S(2)}) copy-start(bf16[256,1024]{1,0:T(8,128)(2,1)} %x_ref) | copy-start | bytes 1572868
  43.9 11.2 %all-to-all-start.2 = ((f32[16,16,128]{2,1,0:T(8,128)}), f32[16,16,128]{2,1,0:T(8,128)S(1)}, u32[]{:S(2)}, u32[]{:S(2)}) async-start(f32[16,16,128]{2,1,0:T(8,128)} %relay.1), calls=%async_computation.2 | async-start | bytes 262144 | tf_op jit(solution)/shard_map/all_to_all | solution.py:328
  50.1 1.0 %copy-start.1 = (bf16[256,1024]{1,0:T(8,128)(2,1)S(1)}, bf16[256,1024]{1,0:T(8,128)(2,1)}, u32[]{:S(2)}) copy-start(bf16[256,1024]{1,0:T(8,128)(2,1)} %x_ref.1) | copy-start | bytes 1572868
  51.2 3.9 %copy-start.3 = (f32[16,1024]{1,0:T(8,128)S(1)}, f32[16,1024]{1,0:T(8,128)}, u32[]{:S(2)}) copy-start(f32[16,1024]{1,0:T(8,128)} %rate_ref.1) | copy-start | bytes 196612

commit v7 on v6

--- a/solution.py
+++ b/solution.py
@@ -6,7 +6,6 @@
 from jax.experimental.pallas import tpu as pltpu
 from jax.sharding import PartitionSpec as P
 
-PARTS = 4
 SUB = 8
 LANES = 128
 F32 = jnp.float32
@@ -18,6 +17,27 @@
 
 def block_index():
     return lax.broadcasted_iota(jnp.int32, (SUB, LANES), 0)
+
+
+def summed_positions(parts):
+    at = block_index()
+    low = at < 4
+    parts = [
+        jnp.where(low, parts[i], parts[i + 4])
+        + pltpu.roll(jnp.where(low, parts[i + 4], parts[i]), 4, 0)
+        for i in range(4)
+    ]
+    for by in (2, 1):
+        low = lax.rem(at, 2 * by) < by
+        parts = [
+            jnp.where(
+                low,
+                parts[i] + pltpu.roll(parts[i], SUB - by, 0),
+                parts[i + by] + pltpu.roll(parts[i + by], by, 0),
+            )
+            for i in range(by)
+        ]
+    return parts[0]
 
 
 def ends_kernel(
@@ -28,70 +48,69 @@
     signal_ref,
     cotangent_ref,
     rate_ref,
-    turned_ref,
-    decays_ref,
     sems,
     rate_sem,
 ):
     positions, width = signal_ref.shape
     states = rate_ref.shape[0]
-    columns = width // LANES
-    pair = 2 * SUB
-    share = positions // PARTS
+    tiles = positions // SUB
 
     def part_copies(part):
-        copies = []
-        for side, (hbm, ref) in enumerate(
-            ((signal_hbm, signal_ref), (cotangent_hbm, cotangent_ref))
-        ):
-            at = part if side == 0 else PARTS - 1 - part
-            rows = pl.ds(pl.multiple_of(at * share, share), share)
-            copies.append(
-                pltpu.make_async_copy(hbm.at[rows, :], ref.at[rows, :], sems.at[side, part])
+        lanes = pl.ds(pl.multiple_of(part * 2 * LANES, 2 * LANES), 2 * LANES)
+        return [
+            pltpu.make_async_copy(hbm.at[:, lanes], ref.at[:, lanes], sems.at[side, part])
+            for side, (hbm, ref) in enumerate(
+                ((signal_hbm, signal_ref), (cotangent_hbm, cotangent_ref))
             )
-        return copies
+        ]
 
     rate_copy = pltpu.make_async_copy(rate_hbm, rate_ref, rate_sem)
     rate_copy.start()
-    for part in range(PARTS):
+    for part in range(width // (2 * LANES)):
         for copy in part_copies(part):
             copy.start()
     rate_copy.wait()
-    for c in range(columns):
-        rate = rate_ref[:, c * LANES : (c + 1) * LANES]
-        decays_ref[pl.ds(c, states, stride=columns), :] = jnp.exp(-rate)
-    decay = [decays_ref[n * columns : (n + 1) * columns, :] for n in range(states)]
-
-    def advance(step, state):
-        start = pl.multiple_of(step * pair, pair)
-        last = pl.multiple_of(positions - pair - step * pair, pair)
-        for c in range(columns):
-            lanes = pl.ds(c * LANES, LANES)
-            x = signal_ref[pl.ds(start, pair), lanes]
-            turned_ref[0, pl.ds(c, pair, stride=columns), :] = x.astype(F32)
-            g = cotangent_ref[pl.ds(last, pair), lanes]
-            turned_ref[1, pl.ds(c, pair, stride=columns), :] = g.astype(F32)
-        ends, starts = list(state[0]), list(state[1])
-        for t in range(pair):
-            x = turned_ref[0, t * columns : (t + 1) * columns, :]
-            back = pair - 1 - t
-            g = turned_ref[1, back * columns : (back + 1) * columns, :]
-            for n in range(states):
-                ends[n] = decay[n] * ends[n] + x
-                starts[n] = decay[n] * starts[n] + g
-        return tuple(ends), tuple(starts)
-
-    def part_of(part, state):
+    place = block_index()
+    after = (SUB - 1 - place).astype(F32)
+    before = place.astype(F32)
+
+    def column(c, _):
+        lanes = pl.ds(pl.multiple_of(c * LANES, LANES), LANES)
+        rate = rate_ref[:, lanes]
+        decay_table = jnp.exp(-rate * float(SUB))
+        decay = [row_of(decay_table, n) for n in range(states)]
+        ends = [None] * states
+        starts = [None] * states
+        for pair in range(tiles // 2):
+            first = pair * 2 * SUB
+            x = signal_ref[first : first + 2 * SUB, lanes].astype(F32)
+            last = positions - 2 * SUB - first
+            g = cotangent_ref[last : last + 2 * SUB, lanes].astype(F32)
+            for half in range(2):
+                xh = x[half * SUB : (half + 1) * SUB]
+                gh = g[(1 - half) * SUB : (2 - half) * SUB]
+                for n in range(states):
+                    if pair == 0 and half == 0:
+                        ends[n], starts[n] = xh, gh
+                    else:
+                        ends[n] = decay[n] * ends[n] + xh
+                        starts[n] = decay[n] * starts[n] + gh
+        for side, (sums, distance) in enumerate(((ends, after), (starts, before))):
+            for low in range(0, states, SUB):
+                parts = [
+                    jnp.exp(-row_of(rate, n) * distance) * sums[n]
+                    for n in range(low, low + SUB)
+                ]
+                at = pl.ds(pl.multiple_of(c * states + low, SUB), SUB)
+                ends_ref[side, at, :] = summed_positions(parts)
+        return 0
+
+    def both_columns(part, _):
         for copy in part_copies(part):
             copy.wait()
-        steps = share // pair
-        return lax.fori_loop(part * steps, (part + 1) * steps, advance, state)
-
-    zero = (jnp.zeros((columns, LANES), F32),) * states
-    sums = lax.fori_loop(0, PARTS, part_of, (zero, zero))
-    for side in range(2):
-        for n in range(states):
-            ends_ref[side, n * columns : (n + 1) * columns, :] = sums[side][n]
+        return lax.fori_loop(2 * part, 2 * part + 2, column, 0)
+
+    lax.fori_loop(0, width // (2 * LANES), both_columns, 0)
 
 
 def within_kernel(is_forward, x_ref, table_ref, *refs):
@@ -249,7 +268,7 @@
         lanes = pl.ds(pl.multiple_of(c * LANES, LANES), LANES)
         decay_table = jnp.exp(-rate_ref[:, lanes] * float(SUB))
         decay = [row_of(decay_table, n) for n in range(states)]
-        rows = pl.ds(c, states, stride=width // LANES)
+        rows = pl.ds(pl.multiple_of(c * states, states), states)
         for side, result in enumerate((out_ref, grad_ref)):
             local_ref = both_ref.at[side]
             carried = carried_ref[side, rows, :]
@@ -310,9 +329,7 @@
             whole,
             whole,
             pltpu.VMEM(decay_rate.shape, F32),
-            pltpu.VMEM((2, 2 * SUB * columns, LANES), F32),
-            turned,
-            pltpu.SemaphoreType.DMA((2, PARTS)),
+            copy_sems,
             pltpu.SemaphoreType.DMA,
         ],
         compiler_params=vmem(56),
@@ -329,7 +346,8 @@
 
     gathered = exchanged(ends.reshape(layout.members, rows, LANES), layout.member_groups())
     rate_then, _ = lax.optimization_barrier((decay_rate, ends))
-    span = jnp.exp(-float(positions) * rate_then).reshape(states * columns, LANES)
+    span = jnp.exp(-float(positions) * rate_then).reshape(states, columns, LANES)
+    span = span.swapaxes(0, 1).reshape(columns * states, LANES)
     weight = residue * jnp.sqrt(-jnp.expm1(-2.0 * rate_then))
     tables = jnp.concatenate([rate_then, weight, skip_gain.reshape(1, channels)], axis=0)
     span, tables = lax.optimization_barrier((span, tables))
@@ -374,7 +392,7 @@
         in_specs=[in_smem] + [in_vmem] * 3,
         out_specs=in_vmem,
         out_shape=jax.ShapeDtypeStruct((layout.members, rows, LANES), F32),
-        compiler_params=vmem(56),
+        compiler_params=vmem(4),
         name="relay",
     )(index, gathered, peers, span)
     cotangent, _ = lax.optimization_barrier((cotangent, carried))

time: 58.9 us -> 58.2 us (0.988)
  Pallas kernels: 16.4 us -> 15.1 us
  local copies, waits for them, and re-layouts: 2.11 us -> 2.74 us
    pallas_call x1, Pallas kernels: 1.68 us -> 0.96 us  [shards(): pl.pallas_call(functools.partial(relay_kernel, layout), in_specs=[in_smem...]
    unnamed x10 -> x8, local copies, waits for them, and re-layouts: 2.09 us -> 2.73 us
    pallas_call x1, Pallas kernels: 5.27 us -> 4.65 us  [shards(): pl.pallas_call(ends_kernel, in_specs=[in_hbm] * 3, out_specs=in_vmem, out...]
where the time goes in v7:
time: 58.2 us; the launch traced here: 57.6 us
  starting transfers between devices  30.9 us (53%)
  Pallas kernels  15.1 us (26%)
  waiting for transfers between devices  6.46 us (11%)
  local copies, waits for them, and re-layouts  2.74 us (5%)
  other arithmetic  1.8 us (3%)
  between operations  0.68 us (1%)
    all_to_all x3, starting transfers between devices, exchanged(): return lax.all_to_all(x, 'seq', 0, 0, axis_index_groups=groups)  30.9 us
    all_to_all x3, waiting for transfers between devices, exchanged(): return lax.all_to_all(x, 'seq', 0, 0, axis_index_groups=groups)  6.46 us
    pallas_call x2, Pallas kernels, within(): pl.pallas_call(functools.partial(within_kernel, is_forward), in_specs=[in...  5.6 us
    pallas_call x1, Pallas kernels, shards(): pl.pallas_call(ends_kernel, in_specs=[in_hbm] * 3, out_specs=in_vmem, out...  4.65 us
    pallas_call x1, Pallas kernels, shards(): pl.pallas_call(carry_kernel, in_specs=[in_vmem] * 3, out_specs=[in_hbm] *...  3.18 us
    unnamed x8, local copies, waits for them, and re-layouts  2.73 us
  transfers between devices with their start and end apart: 3, of which 3 were waited for; matrix products, arithmetic and copies ran while one was open for 3% of the time, Pallas kernels for 10%

profile of v7, /device:TPU:24, one launch (start us, length us, event | category | flops | bytes accessed | tf_op | source)
XLA Modules:
  0.0 57.6 jit_solution(7280057815593830342)
XLA Ops:
  0.6 4.6 %ends.1 = f32[2,128,128]{2,1,0:T(8,128)} custom-call(bf16[256,1024]{1,0:T(8,128)(2,1)} %x_ref, bf16[256,1024]{1,0:T(8,128)(2,1)} %x_ref.1, f32[16,1024]{1,0:T(8,128)} %rate_ref.1), custom_call_target="tpu_custom_call" | custom-call | tf_op jit(solution)/shard_map/ends/pallas_call | solution.py:323
  5.3 9.6 %all-to-all-start = ((f32[16,16,128]{2,1,0:T(8,128)}), f32[16,16,128]{2,1,0:T(8,128)S(1)}, u32[]{:S(2)}, u32[]{:S(2)}) async-start(f32[16,16,128]{2,1,0:T(8,128)} %bitcast.15), calls=%async_computation | async-start | bytes 262144 | tf_op jit(solution)/shard_map/all_to_all | solution.py:345
  14.9 0.9 %sqrt_multiply_fusion = (f32[16,1024]{1,0:T(8,128)S(1)}, f32[2,8,8,128]{3,2,1,0:T(8,128)S(1)}) fusion(f32[16,1024]{1,0:T(8,128)} %param.8, f32[16,1024]{1,0:T(8,128)} %rate_ref.1), kind=kLoop, calls=%fused_computation.2 | loop fusion | flops 65536 | bytes 262144 | tf_op jit(solution)/shard_map/mul | solution.py:351
  15.8 0.9 %pad_maximum_fusion.table_ref = f32[33,1024]{1,0:T(8,128)S(1)} fusion(f32[1,1024]{1,0:T(1,128)} %bitcast.16, f32[16,1024]{1,0:T(8,128)S(1)} %get-tuple-element.16, f32[16,1024]{1,0:T(8,128)} %rate_ref.1), kind=kLoop, calls=%fused_computation | loop fusion | flops 67584 | bytes 270336 | tf_op jit(solution)/shard_map/concatenate | solution.py:352
  16.7 3.2 %all-to-all-done.ends_ref = f32[16,16,128]{2,1,0:T(8,128)S(1)} async-done(((f32[16,16,128]{2,1,0:T(8,128)}), f32[16,16,128]{2,1,0:T(8,128)S(1)}, u32[]{:S(2)}, u32[]{:S(2)}) %all-to-all-start) | async-done | bytes 131104 | tf_op jit(solution)/shard_map/all_to_all | solution.py:345
  19.9 0.7 %totals.1 = f32[4,4,16,128]{3,2,1,0:T(8,128)} custom-call(s32[1]{0:T(128)} %bitcast.index_ref, f32[16,16,128]{2,1,0:T(8,128)S(1)} %all-to-all-done.ends_ref, f32[128,128]{1,0:T(8,128)S(1)} %bitcast.12), custom_call_target="tpu_custom_call" | custom-call | tf_op jit(solution)/shard_map/totals/pallas_call | solution.py:354
  20.5 15.0 %all-to-all-start.1 = ((f32[4,4,16,128]{3,2,1,0:T(8,128)}), f32[4,4,16,128]{3,2,1,0:T(8,128)}, u32[]{:S(2)}, u32[]{:S(2)}) async-start(f32[4,4,16,128]{3,2,1,0:T(8,128)} %totals.1), calls=%async_computation.1 | async-start | bytes 262144 | tf_op jit(solution)/shard_map/all_to_all | solution.py:345
  35.6 0.0 copy-start
  35.6 1.0 %copy-done = bf16[256,1024]{1,0:T(8,128)(2,1)S(1)} copy-done((bf16[256,1024]{1,0:T(8,128)(2,1)S(1)}, bf16[256,1024]{1,0:T(8,128)(2,1)}, u32[]{:S(2)}) %copy-start) | copy-done | bytes 524312
  36.6 2.8 %within_forward.1.refs_0_ = f32[2,384,1024]{2,1,0:T(8,128)S(1)} custom-call(bf16[256,1024]{1,0:T(8,128)(2,1)S(1)} %copy-done, f32[33,1024]{1,0:T(8,128)S(1)} %pad_maximum_fusion.table_ref), custom_call_target="tpu_custom_call" | custom-call | flops 25165824 | bytes 1572864 | tf_op jit(solution)/shard_map/within_forward/pallas_call | solution.py:367
  39.4 2.2 %all-to-all-done.1.totals_ref = f32[4,4,16,128]{3,2,1,0:T(8,128)} async-done(((f32[4,4,16,128]{3,2,1,0:T(8,128)}), f32[4,4,16,128]{3,2,1,0:T(8,128)}, u32[]{:S(2)}, u32[]{:S(2)}) %all-to-all-start.1) | async-done | bytes 131104 | tf_op jit(solution)/shard_map/all_to_all | solution.py:345
  41.6 1.0 %relay.1 = f32[16,16,128]{2,1,0:T(8,128)S(1)} custom-call(s32[1]{0:T(128)} %bitcast.index_ref, f32[16,16,128]{2,1,0:T(8,128)S(1)} %all-to-all-done.ends_ref, f32[4,4,16,128]{3,2,1,0:T(8,128)} %all-to-all-done.1.totals_ref, f32[128,128]{1,0:T(8,128)S(1)} %bitcast.13), custom_call_target="tpu_custom_call" | custom-call | tf_op jit(solution)/shard_map/relay/pallas_call | solution.py:390
  42.5 0.0 copy-start.3
  42.5 0.6 %copy-done.3 = f32[16,16,128]{2,1,0:T(8,128)} copy-done((f32[16,16,128]{2,1,0:T(8,128)}, f32[16,16,128]{2,1,0:T(8,128)S(1)}, u32[]{:S(2)}) %copy-start.3) | copy-done | bytes 131096
  43.2 6.2 %all-to-all-start.2 = ((f32[16,16,128]{2,1,0:T(8,128)}), f32[16,16,128]{2,1,0:T(8,128)S(1)}, u32[]{:S(2)}, u32[]{:S(2)}) async-start(f32[16,16,128]{2,1,0:T(8,128)} %copy-done.3), calls=%async_computation.2 | async-start | bytes 262144 | tf_op jit(solution)/shard_map/all_to_all | solution.py:345
  49.4 0.0 copy-start.1
  49.4 1.0 %copy-done.1 = bf16[256,1024]{1,0:T(8,128)(2,1)S(1)} copy-done((bf16[256,1024]{1,0:T(8,128)(2,1)S(1)}, bf16[256,1024]{1,0:T(8,128)(2,1)}, u32[]{:S(2)}) %copy-start.1) | copy-done | bytes 524312
  50.5 0.0 copy-start.2
  50.5 2.8 %within_backward.1.both_ref = f32[2,384,1024]{2,1,0:T(8,128)S(1)} custom-call(bf16[256,1024]{1,0:T(8,128)(2,1)S(1)} %copy-done.1, f32[33,1024]{1,0:T(8,128)S(1)} %pad_maximum_fusion.table_ref, f32[2,384,1024]{2,1,0:T(8,128)S(1)} %within_forward.1.refs_0_), custom_call_target="tpu_custom_call", output_to_operand_aliasing={{}: (2, {})} | custom-call | flops 25165824 | bytes 1572864 | tf_op jit(solution)/shard_map/within_backward/pallas_call | solution.py:367
  53.3 1.1 %all-to-all-done.2 = f32[16,16,128]{2,1,0:T(8,128)S(1)} async-done(((f32[16,16,128]{2,1,0:T(8,128)}), f32[16,16,128]{2,1,0:T(8,128)S(1)}, u32[]{:S(2)}, u32[]{:S(2)}) %all-to-all-start.2) | async-done | bytes 131104 | tf_op jit(solution)/shard_map/all_to_all | solution.py:345
  54.4 0.0 copy-done.2
  54.4 3.2 %carry.1 = (bf16[256,1024]{1,0:T(8,128)(2,1)}, bf16[256,1024]{1,0:T(8,128)(2,1)}) custom-call(f32[2,384,1024]{2,1,0:T(8,128)S(1)} %within_backward.1.both_ref, f32[16,1024]{1,0:T(8,128)S(1)} %copy-done.2, f32[2,128,128]{2,1,0:T(8,128)S(1)} %bitcast.14), custom_call_target="tpu_custom_call" | custom-call | tf_op jit(solution)/shard_map/carry/pallas_call | solution.py:403
  (1 shorter events, 0.0 us)
Async XLA Ops:
  5.3 14.6 %all-to-all-start = ((f32[16,16,128]{2,1,0:T(8,128)}), f32[16,16,128]{2,1,0:T(8,128)S(1)}, u32[]{:S(2)}, u32[]{:S(2)}) async-start(f32[16,16,128]{2,1,0:T(8,128)} %bitcast.15), calls=%async_computation | async-start | bytes 262144 | tf_op jit(solution)/shard_map/all_to_all | solution.py:345
  20.5 21.0 %all-to-all-start.1 = ((f32[4,4,16,128]{3,2,1,0:T(8,128)}), f32[4,4,16,128]{3,2,1,0:T(8,128)}, u32[]{:S(2)}, u32[]{:S(2)}) async-start(f32[4,4,16,128]{3,2,1,0:T(8,128)} %totals.1), calls=%async_computation.1 | async-start | bytes 262144 | tf_op jit(solution)/shard_map/all_to_all | solution.py:345
  35.6 1.0 %copy-start = (bf16[256,1024]{1,0:T(8,128)(2,1)S(1)}, bf16[256,1024]{1,0:T(8,128)(2,1)}, u32[]{:S(2)}) copy-start(bf16[256,1024]{1,0:T(8,128)(2,1)} %x_ref) | copy-start | bytes 1572868
  42.5 0.7 %copy-start.3 = (f32[16,16,128]{2,1,0:T(8,128)}, f32[16,16,128]{2,1,0:T(8,128)S(1)}, u32[]{:S(2)}) copy-start(f32[16,16,128]{2,1,0:T(8,128)S(1)} %relay.1) | copy-start | bytes 393220
  43.2 11.2 %all-to-all-start.2 = ((f32[16,16,128]{2,1,0:T(8,128)}), f32[16,16,128]{2,1,0:T(8,128)S(1)}, u32[]{:S(2)}, u32[]{:S(2)}) async-start(f32[16,16,128]{2,1,0:T(8,128)} %copy-done.3), calls=%async_computation.2 | async-start | bytes 262144 | tf_op jit(solution)/shard_map/all_to_all | solution.py:345
  49.4 1.0 %copy-start.1 = (bf16[256,1024]{1,0:T(8,128)(2,1)S(1)}, bf16[256,1024]{1,0:T(8,128)(2,1)}, u32[]{:S(2)}) copy-start(bf16[256,1024]{1,0:T(8,128)(2,1)} %x_ref.1) | copy-start | bytes 1572868
  50.5 3.9 %copy-start.2 = (f32[16,1024]{1,0:T(8,128)S(1)}, f32[16,1024]{1,0:T(8,128)}, u32[]{:S(2)}) copy-start(f32[16,1024]{1,0:T(8,128)} %rate_ref.1) | copy-start | bytes 196612

commit v8 on v7

--- a/solution.py
+++ b/solution.py
@@ -135,7 +135,7 @@
             local_ref[pl.ds(positions + n * SUB, SUB), lanes] = row_of(weight, n) * reach
     decay = [decays_ref[n * columns : (n + 1) * columns, :] for n in range(states)]
     weight = [weights_ref[n * columns : (n + 1) * columns, :] for n in range(states)]
-    gain = gains_ref[...]
+    gain = gains_ref[:columns]
 
     def advance(step, state):
         at = step if is_forward else positions // pair - 1 - step
@@ -317,7 +317,7 @@
     in_vmem = pl.BlockSpec(memory_space=pltpu.VMEM)
     elements = positions * channels * states
     whole = pltpu.VMEM((positions, channels), signal.dtype)
-    turned = pltpu.VMEM((states * columns, LANES), F32)
+    turned = pltpu.VMEM(((states + 1) * columns, LANES), F32)
     copy_sems = pltpu.SemaphoreType.DMA((2, columns // 2))
 
     ends = pl.pallas_call(
@@ -371,10 +371,10 @@
             out_shape=jax.ShapeDtypeStruct((2, depth, channels), F32),
             input_output_aliases={2: 0} if other else {},
             scratch_shapes=[
-                pltpu.VMEM((2 * SUB * columns, LANES), F32),
+                pltpu.VMEM(((2 * SUB + 1) * columns, LANES), F32),
                 turned,
                 turned,
-                pltpu.VMEM((columns, LANES), F32),
+                pltpu.VMEM((columns + SUB, LANES), F32),
             ],
             cost_estimate=pl.CostEstimate(
                 flops=6 * elements, bytes_accessed=6 * positions * channels, transcendentals=0

time: 58.2 us -> 58.2 us (level)
  no operation moved by 1% of the time
where the time goes in v8:
time: 58.2 us; the launch traced here: 57.6 us
  starting transfers between devices  30.9 us (53%)
  Pallas kernels  15.1 us (26%)
  waiting for transfers between devices  6.46 us (11%)
  local copies, waits for them, and re-layouts  2.74 us (5%)
  other arithmetic  1.8 us (3%)
  between operations  0.68 us (1%)
    all_to_all x3, starting transfers between devices, exchanged(): return lax.all_to_all(x, 'seq', 0, 0, axis_index_groups=groups)  30.9 us
    all_to_all x3, waiting for transfers between devices, exchanged(): return lax.all_to_all(x, 'seq', 0, 0, axis_index_groups=groups)  6.46 us
    pallas_call x2, Pallas kernels, within(): pl.pallas_call(functools.partial(within_kernel, is_forward), in_specs=[in...  5.6 us
    pallas_call x1, Pallas kernels, shards(): pl.pallas_call(ends_kernel, in_specs=[in_hbm] * 3, out_specs=in_vmem, out...  4.65 us
    pallas_call x1, Pallas kernels, shards(): pl.pallas_call(carry_kernel, in_specs=[in_vmem] * 3, out_specs=[in_hbm] *...  3.18 us
    unnamed x8, local copies, waits for them, and re-layouts  2.73 us
  transfers between devices with their start and end apart: 3, of which 3 were waited for; matrix products, arithmetic and copies ran while one was open for 3% of the time, Pallas kernels for 10%

profile of v8, /device:TPU:24, one launch (start us, length us, event | category | flops | bytes accessed | tf_op | source)
XLA Modules:
  0.0 57.6 jit_solution(382469842582037013)
XLA Ops:
  0.6 4.6 %ends.1 = f32[2,128,128]{2,1,0:T(8,128)} custom-call(bf16[256,1024]{1,0:T(8,128)(2,1)} %x_ref, bf16[256,1024]{1,0:T(8,128)(2,1)} %x_ref.1, f32[16,1024]{1,0:T(8,128)} %rate_ref.1), custom_call_target="tpu_custom_call" | custom-call | tf_op jit(solution)/shard_map/ends/pallas_call | solution.py:323
  5.3 9.6 %all-to-all-start = ((f32[16,16,128]{2,1,0:T(8,128)}), f32[16,16,128]{2,1,0:T(8,128)S(1)}, u32[]{:S(2)}, u32[]{:S(2)}) async-start(f32[16,16,128]{2,1,0:T(8,128)} %bitcast.15), calls=%async_computation | async-start | bytes 262144 | tf_op jit(solution)/shard_map/all_to_all | solution.py:345
  14.9 0.9 %sqrt_multiply_fusion = (f32[16,1024]{1,0:T(8,128)S(1)}, f32[2,8,8,128]{3,2,1,0:T(8,128)S(1)}) fusion(f32[16,1024]{1,0:T(8,128)} %param.8, f32[16,1024]{1,0:T(8,128)} %rate_ref.1), kind=kLoop, calls=%fused_computation.2 | loop fusion | flops 65536 | bytes 262144 | tf_op jit(solution)/shard_map/mul | solution.py:351
  15.8 0.9 %pad_maximum_fusion.table_ref = f32[33,1024]{1,0:T(8,128)S(1)} fusion(f32[1,1024]{1,0:T(1,128)} %bitcast.16, f32[16,1024]{1,0:T(8,128)S(1)} %get-tuple-element.16, f32[16,1024]{1,0:T(8,128)} %rate_ref.1), kind=kLoop, calls=%fused_computation | loop fusion | flops 67584 | bytes 270336 | tf_op jit(solution)/shard_map/concatenate | solution.py:352
  16.7 3.2 %all-to-all-done.ends_ref = f32[16,16,128]{2,1,0:T(8,128)S(1)} async-done(((f32[16,16,128]{2,1,0:T(8,128)}), f32[16,16,128]{2,1,0:T(8,128)S(1)}, u32[]{:S(2)}, u32[]{:S(2)}) %all-to-all-start) | async-done | bytes 131104 | tf_op jit(solution)/shard_map/all_to_all | solution.py:345
  19.9 0.7 %totals.1 = f32[4,4,16,128]{3,2,1,0:T(8,128)} custom-call(s32[1]{0:T(128)} %bitcast.index_ref, f32[16,16,128]{2,1,0:T(8,128)S(1)} %all-to-all-done.ends_ref, f32[128,128]{1,0:T(8,128)S(1)} %bitcast.12), custom_call_target="tpu_custom_call" | custom-call | tf_op jit(solution)/shard_map/totals/pallas_call | solution.py:354
  20.5 15.0 %all-to-all-start.1 = ((f32[4,4,16,128]{3,2,1,0:T(8,128)}), f32[4,4,16,128]{3,2,1,0:T(8,128)}, u32[]{:S(2)}, u32[]{:S(2)}) async-start(f32[4,4,16,128]{3,2,1,0:T(8,128)} %totals.1), calls=%async_computation.1 | async-start | bytes 262144 | tf_op jit(solution)/shard_map/all_to_all | solution.py:345
  35.6 0.0 copy-start
  35.6 1.0 %copy-done = bf16[256,1024]{1,0:T(8,128)(2,1)S(1)} copy-done((bf16[256,1024]{1,0:T(8,128)(2,1)S(1)}, bf16[256,1024]{1,0:T(8,128)(2,1)}, u32[]{:S(2)}) %copy-start) | copy-done | bytes 524312
  36.6 2.8 %within_forward.1.refs_0_ = f32[2,384,1024]{2,1,0:T(8,128)S(1)} custom-call(bf16[256,1024]{1,0:T(8,128)(2,1)S(1)} %copy-done, f32[33,1024]{1,0:T(8,128)S(1)} %pad_maximum_fusion.table_ref), custom_call_target="tpu_custom_call" | custom-call | flops 25165824 | bytes 1572864 | tf_op jit(solution)/shard_map/within_forward/pallas_call | solution.py:367
  39.4 2.2 %all-to-all-done.1.totals_ref = f32[4,4,16,128]{3,2,1,0:T(8,128)} async-done(((f32[4,4,16,128]{3,2,1,0:T(8,128)}), f32[4,4,16,128]{3,2,1,0:T(8,128)}, u32[]{:S(2)}, u32[]{:S(2)}) %all-to-all-start.1) | async-done | bytes 131104 | tf_op jit(solution)/shard_map/all_to_all | solution.py:345
  41.6 1.0 %relay.1 = f32[16,16,128]{2,1,0:T(8,128)S(1)} custom-call(s32[1]{0:T(128)} %bitcast.index_ref, f32[16,16,128]{2,1,0:T(8,128)S(1)} %all-to-all-done.ends_ref, f32[4,4,16,128]{3,2,1,0:T(8,128)} %all-to-all-done.1.totals_ref, f32[128,128]{1,0:T(8,128)S(1)} %bitcast.13), custom_call_target="tpu_custom_call" | custom-call | tf_op jit(solution)/shard_map/relay/pallas_call | solution.py:390
  42.5 0.0 copy-start.3
  42.5 0.6 %copy-done.3 = f32[16,16,128]{2,1,0:T(8,128)} copy-done((f32[16,16,128]{2,1,0:T(8,128)}, f32[16,16,128]{2,1,0:T(8,128)S(1)}, u32[]{:S(2)}) %copy-start.3) | copy-done | bytes 131096
  43.2 6.2 %all-to-all-start.2 = ((f32[16,16,128]{2,1,0:T(8,128)}), f32[16,16,128]{2,1,0:T(8,128)S(1)}, u32[]{:S(2)}, u32[]{:S(2)}) async-start(f32[16,16,128]{2,1,0:T(8,128)} %copy-done.3), calls=%async_computation.2 | async-start | bytes 262144 | tf_op jit(solution)/shard_map/all_to_all | solution.py:345
  49.4 0.0 copy-start.1
  49.4 1.0 %copy-done.1 = bf16[256,1024]{1,0:T(8,128)(2,1)S(1)} copy-done((bf16[256,1024]{1,0:T(8,128)(2,1)S(1)}, bf16[256,1024]{1,0:T(8,128)(2,1)}, u32[]{:S(2)}) %copy-start.1) | copy-done | bytes 524312
  50.5 0.0 copy-start.2
  50.5 2.8 %within_backward.1.both_ref = f32[2,384,1024]{2,1,0:T(8,128)S(1)} custom-call(bf16[256,1024]{1,0:T(8,128)(2,1)S(1)} %copy-done.1, f32[33,1024]{1,0:T(8,128)S(1)} %pad_maximum_fusion.table_ref, f32[2,384,1024]{2,1,0:T(8,128)S(1)} %within_forward.1.refs_0_), custom_call_target="tpu_custom_call", output_to_operand_aliasing={{}: (2, {})} | custom-call | flops 25165824 | bytes 1572864 | tf_op jit(solution)/shard_map/within_backward/pallas_call | solution.py:367
  53.3 1.1 %all-to-all-done.2 = f32[16,16,128]{2,1,0:T(8,128)S(1)} async-done(((f32[16,16,128]{2,1,0:T(8,128)}), f32[16,16,128]{2,1,0:T(8,128)S(1)}, u32[]{:S(2)}, u32[]{:S(2)}) %all-to-all-start.2) | async-done | bytes 131104 | tf_op jit(solution)/shard_map/all_to_all | solution.py:345
  54.4 0.0 copy-done.2
  54.4 3.2 %carry.1 = (bf16[256,1024]{1,0:T(8,128)(2,1)}, bf16[256,1024]{1,0:T(8,128)(2,1)}) custom-call(f32[2,384,1024]{2,1,0:T(8,128)S(1)} %within_backward.1.both_ref, f32[16,1024]{1,0:T(8,128)S(1)} %copy-done.2, f32[2,128,128]{2,1,0:T(8,128)S(1)} %bitcast.14), custom_call_target="tpu_custom_call" | custom-call | tf_op jit(solution)/shard_map/carry/pallas_call | solution.py:403
  (1 shorter events, 0.0 us)
Async XLA Ops:
  5.3 14.6 %all-to-all-start = ((f32[16,16,128]{2,1,0:T(8,128)}), f32[16,16,128]{2,1,0:T(8,128)S(1)}, u32[]{:S(2)}, u32[]{:S(2)}) async-start(f32[16,16,128]{2,1,0:T(8,128)} %bitcast.15), calls=%async_computation | async-start | bytes 262144 | tf_op jit(solution)/shard_map/all_to_all | solution.py:345
  20.5 21.0 %all-to-all-start.1 = ((f32[4,4,16,128]{3,2,1,0:T(8,128)}), f32[4,4,16,128]{3,2,1,0:T(8,128)}, u32[]{:S(2)}, u32[]{:S(2)}) async-start(f32[4,4,16,128]{3,2,1,0:T(8,128)} %totals.1), calls=%async_computation.1 | async-start | bytes 262144 | tf_op jit(solution)/shard_map/all_to_all | solution.py:345
  35.6 1.0 %copy-start = (bf16[256,1024]{1,0:T(8,128)(2,1)S(1)}, bf16[256,1024]{1,0:T(8,128)(2,1)}, u32[]{:S(2)}) copy-start(bf16[256,1024]{1,0:T(8,128)(2,1)} %x_ref) | copy-start | bytes 1572868
  42.5 0.7 %copy-start.3 = (f32[16,16,128]{2,1,0:T(8,128)}, f32[16,16,128]{2,1,0:T(8,128)S(1)}, u32[]{:S(2)}) copy-start(f32[16,16,128]{2,1,0:T(8,128)S(1)} %relay.1) | copy-start | bytes 393220
  43.2 11.2 %all-to-all-start.2 = ((f32[16,16,128]{2,1,0:T(8,128)}), f32[16,16,128]{2,1,0:T(8,128)S(1)}, u32[]{:S(2)}, u32[]{:S(2)}) async-start(f32[16,16,128]{2,1,0:T(8,128)} %copy-done.3), calls=%async_computation.2 | async-start | bytes 262144 | tf_op jit(solution)/shard_map/all_to_all | solution.py:345
  49.4 1.0 %copy-start.1 = (bf16[256,1024]{1,0:T(8,128)(2,1)S(1)}, bf16[256,1024]{1,0:T(8,128)(2,1)}, u32[]{:S(2)}) copy-start(bf16[256,1024]{1,0:T(8,128)(2,1)} %x_ref.1) | copy-start | bytes 1572868
  50.5 3.9 %copy-start.2 = (f32[16,1024]{1,0:T(8,128)S(1)}, f32[16,1024]{1,0:T(8,128)}, u32[]{:S(2)}) copy-start(f32[16,1024]{1,0:T(8,128)} %rate_ref.1) | copy-start | bytes 196612
